TPU v7x, 128 devices: a whole 4x4x4 slice. The times are simulated.
128 devices in a mesh: row: 8 (over y_hi, z), col: 16 (over x, y_lo, core).
Axes of the slice: x: 4, y: 4 (y_hi: 2, y_lo: 2; y = y_hi * 2 + y_lo), z: 4, core: 2. Of those that a mesh axis runs over, the one named last changes fastest.
Arguments:
- ancestor_inv: float32 [12288, 12288], P('row', 'col'), as said below
- lower_panel: float32 [12288, 4096], P(None, 'col'), may hold values from -1.5 to 1.5
- diag_block_inv: float32 [32, 128, 128], P('col', 'row'), as said below
- pattern: int32 [96, 32], replicated, may hold values 0 or 1
Outputs:
- off_inv: float32 [4096, 12288], P('col', 'row')
- diag_inv: float32 [32, 128, 128], P('col', 'row')
Inputs may be any that keep to these rules, and one draw needn't show every extreme that they name: ancestor_inv is symmetric. Each supernode's block of diag_block_inv is symmetric.
All inputs are finite; a program needn't handle non-finite values.
Results may differ from a plain program's by a relative error of at most 0.00007.
Values sent between devices are 32-bit elements; how exact they have to be, the bound alone decides.
A program may use at most 256 MiB of HBM per device.

v0:
```python
import jax
import jax.numpy as jnp
from jax import lax
from jax.sharding import PartitionSpec as P

SUPER = 128


def body(ancestor_inv, lower_panel, diag_block_inv, pattern):
    rows_here, cols_here = ancestor_inv.shape
    full_rows, width_here = lower_panel.shape
    node_count = width_here // SUPER
    block_count = full_rows // SUPER
    col_index = lax.axis_index("col")
    row_index = lax.axis_index("row")
    local_pattern = lax.dynamic_slice_in_dim(pattern, col_index * node_count, node_count, 1).astype(
        jnp.float32
    )
    masked = (
        lower_panel.reshape(block_count, SUPER, node_count, SUPER) * local_pattern[:, None, :, None]
    ).reshape(full_rows, width_here)
    relaid = lax.all_to_all(masked, "col", split_axis=0, concat_axis=1, tiled=True)
    product = lax.psum_scatter(
        lax.dot_general(
            relaid,
            ancestor_inv,
            (((0,), (1,)), ((), ())),
            precision=lax.Precision.HIGHEST,
            preferred_element_type=jnp.float32,
        ),
        "col",
        scatter_dimension=0,
        tiled=True,
    )
    row_blocks = rows_here // SUPER
    kept_rows = lax.dynamic_slice_in_dim(local_pattern, row_index * row_blocks, row_blocks, 0)
    off_inv = -(
        product.reshape(node_count, SUPER, row_blocks, SUPER)
        * jnp.transpose(kept_rows)[:, None, :, None]
    ).reshape(width_here, rows_here)
    panel_rows = lax.dynamic_slice_in_dim(masked, row_index * rows_here, rows_here, 0)
    partial_diag = jnp.einsum(
        "kbg,gkm->kbm",
        product.reshape(node_count, SUPER, rows_here),
        panel_rows.reshape(rows_here, node_count, SUPER),
        precision=lax.Precision.HIGHEST,
        preferred_element_type=jnp.float32,
    )
    summed = lax.psum_scatter(partial_diag, "row", scatter_dimension=1, tiled=True)
    diag_inv = diag_block_inv + summed
    return (off_inv, diag_inv)


def solution(mesh):
    in_specs = (P("row", "col"), P(None, "col"), P("col", "row", None), P())
    out_specs = (P("col", "row"), P("col", "row", None))
    return jax.shard_map(body, mesh=mesh, in_specs=in_specs, out_specs=out_specs, check_vma=False)
```

profile of v0, /device:TPU:2, one launch (start us, length us, event | category | flops | bytes accessed | tf_op | source)
XLA Modules:
  0.0 591.9 jit_solution(3271049572300869253)
XLA Ops:
  7.2 0.0 reduce-scatter.3.cloned.1.call-start
  7.2 0.7 dynamic-slice_convert_fusion
  7.9 0.1 copy.11
  8.0 4.2 mul.32
  12.2 7.6 %bitcast_multiply_fusion = f32[12288,256]{1,0:T(8,128)S(1)} fusion(f32[12288,256]{1,0:T(8,128)} %param.5, f32[1536,8,2,128]{3,2,1,0:T(2,128)S(1)} %bitcast.24), kind=kLoop, calls=%fused_computation | loop fusion | flops 3145728 | bytes 37748736 | tf_op jit(solution)/shard_map/mul | solution.py:20
  19.8 0.0 copy-start
  19.8 143.5 %all_to_all.19 = f32[16,768,256]{2,1,0:T(8,128)} all-to-all(f32[16,768,256]{2,1,0:T(8,128)S(1)} %bitcast.22), channel_id=1, replica_groups=mesh['row'=8,'col'=16] {'col'}, dimensions={0} | all-to-all | bytes 25165824 | tf_op jit(solution)/shard_map/all_to_all | solution.py:22
  163.3 0.0 copy-done
  163.3 12.6 %copy.12 = f32[768,16,256]{0,2,1:T(8,128)} copy(f32[768,16,256]{2,0,1:T(8,128)} %bitcast.23) | data formatting | bytes 25165824 | tf_op jit(solution)/shard_map/all_to_all | solution.py:22
  175.8 66.0 %fusion = f32[4096,1536]{1,0:T(8,128)} fusion(f32[768,4096]{0,1:T(8,128)} %bitcast.25, f32[1536,768]{1,0:T(8,128)} %param.4), kind=kOutput, calls=%fused_computation.6 | convolution fusion | flops 57982058496 | bytes 42467328 | tf_op jit(solution)/shard_map/dot_general | solution.py:24
  241.8 0.0 reduce-scatter.3.cloned.1.call-update
  241.8 0.2 reduce-scatter.5.cloned.1.call-start
  242.1 1.5 constant_dynamic-slice_fusion
  243.6 0.5 copy.15
  244.1 0.1 dynamic-slice_bitcast_fusion
  244.1 0.1 copy.13
  244.2 0.5 mul.36
  244.7 0.1 copy.22
  244.8 1.6 copy.14
  246.4 0.0 copy-start.1
  246.4 255.8 %reduce-scatter.3.cloned.1.call-done = f32[256,1536]{1,0:T(8,128)} async-done(((f32[4096,1536]{1,0:T(8,128)}), f32[256,1536]{1,0:T(8,128)}) %reduce-scatter.3.cloned.1.call-update) | async-done | bytes 1572880 | tf_op jit(solution)/shard_map/reduce_scatter | solution.py:23
  502.3 3.6 fusion.1
  505.9 0.0 reduce-scatter.5.cloned.1.call-update
  505.9 3.3 multiply_negate_fusion
  509.2 74.5 %reduce-scatter.5.cloned.1.call-done = f32[2,16,128]{2,1,0:T(8,128)} async-done(((f32[2,128,128]{2,1,0:T(8,128)}), f32[2,16,128]{2,1,0:T(8,128)}) %reduce-scatter.5.cloned.1.call-update) | async-done | bytes 16400 | tf_op jit(solution)/shard_map/reduce_scatter | solution.py:49
  583.7 0.0 copy-done.1
  583.7 1.3 add.19
Async XLA Ops:
  7.2 495.1 %reduce-scatter.3.cloned.1.call-start = ((), (), s32[]{:S(2)}) async-start(), calls=%async_computation.3 | async-start | bytes 26738688 | tf_op jit(solution)/shard_map/reduce_scatter | solution.py:23
  19.8 143.5 %copy-start = (f32[12288,256]{1,0:T(8,128)}, f32[12288,256]{1,0:T(8,128)S(1)}, u32[]{:S(2)}) copy-start(f32[12288,256]{1,0:T(8,128)S(1)} %bitcast_multiply_fusion) | copy-start | bytes 37748740
  241.8 341.9 %reduce-scatter.5.cloned.1.call-start = ((), (), s32[]{:S(2)}) async-start(), calls=%async_computation.4 | async-start | bytes 147456 | tf_op jit(solution)/shard_map/reduce_scatter | solution.py:49
  246.4 337.3 %copy-start.1 = (f32[2,16,128]{2,1,0:T(8,128)S(1)}, f32[2,16,128]{2,1,0:T(8,128)}, u32[]{:S(2)}) copy-start(f32[2,16,128]{2,1,0:T(8,128)} %param.6) | copy-start | bytes 49156
Sparse Core Ops, SparseCore 0:
  242.0 260.2 reduce-scatter.2
  506.1 77.6 reduce-scatter.4
where the time goes:
time: 592 us
  waiting for transfers between devices  330 us (56%)
  blocking collectives  143 us (24%)
  matrix products  69.6 us (12%)
  local copies, waits for them, and re-layouts  21.2 us (4%)
  between operations  14.1 us (2%)
  other arithmetic  12.9 us (2%)
    reduce_scatter x1, waiting for transfers between devices, body(): lax.psum_scatter(lax.dot_general(relaid, ancestor_inv, (((0,), (1,)), (()...  256 us
    all_to_all x1, blocking collectives, body(): lax.all_to_all(masked, 'col', split_axis=0, concat_axis=1, tiled=True)  143 us
    reduce_scatter x1, waiting for transfers between devices, body(): lax.psum_scatter(partial_diag, 'row', scatter_dimension=1, tiled=True)  74.5 us
    dot_general x1, matrix products, body(): lax.dot_general(relaid, ancestor_inv, (((0,), (1,)), ((), ())), precision...  66 us
    all_to_all x1, local copies, waits for them, and re-layouts, body(): lax.all_to_all(masked, 'col', split_axis=0, concat_axis=1, tiled=True)  12.6 us
  transfers between devices with their start and end apart: 2, of which 2 were waited for; matrix products, arithmetic and copies ran while one was open for 1% of the time, Pallas kernels for 0%

commit v1 on v0

v1 whole, which is shorter than its diff:
```python
import jax
import jax.numpy as jnp
from jax import lax
from jax.sharding import PartitionSpec as P

SUPER = 128


def body(rows, cols, ancestor_inv, lower_panel, diag_block_inv, pattern):
    rows_here, cols_here = ancestor_inv.shape
    full_rows, width_here = lower_panel.shape
    node_count = width_here // SUPER
    row_blocks = rows_here // SUPER
    col_index = lax.axis_index("col")
    row_index = lax.axis_index("row")
    kept = lax.dynamic_slice(
        pattern, (row_index * row_blocks, col_index * node_count), (row_blocks, node_count)
    ).astype(jnp.float32)
    panel_rows = lax.dynamic_slice_in_dim(lower_panel, row_index * rows_here, rows_here, 0)
    masked = (
        panel_rows.reshape(row_blocks, SUPER, node_count, SUPER) * kept[:, None, :, None]
    ).reshape(rows_here, width_here)
    gathered = lax.all_gather(masked, "col", axis=1, tiled=True)
    partial = lax.dot_general(
        gathered,
        ancestor_inv,
        (((0,), (0,)), ((), ())),
        precision=lax.Precision.HIGH,
        preferred_element_type=jnp.float32,
    )
    summed = lax.psum_scatter(partial, "row", scatter_dimension=0, tiled=True)
    odd = col_index % 2
    same, other = [], []
    for r in range(rows):
        for c in range(cols):
            same.append((r * cols + c, (c // 2) * cols + 2 * r + c % 2))
            other.append((r * cols + c, (c // 2) * cols + 2 * r + 1 - c % 2))
    keep_part = lax.dynamic_slice_in_dim(summed, odd * width_here, width_here, 0)
    swap_part = lax.dynamic_slice_in_dim(summed, (1 - odd) * width_here, width_here, 0)
    keep_part = lax.ppermute(keep_part, ("row", "col"), same)
    swap_part = lax.ppermute(swap_part, ("row", "col"), other)
    product = jnp.where(
        odd == 0,
        jnp.concatenate([keep_part, swap_part], 1),
        jnp.concatenate([swap_part, keep_part], 1),
    )
    off_inv = -(
        product.reshape(node_count, SUPER, row_blocks, SUPER) * jnp.transpose(kept)[:, None, :, None]
    ).reshape(width_here, rows_here)
    partial_diag = jnp.einsum(
        "kbg,gkm->kbm",
        product.reshape(node_count, SUPER, rows_here),
        masked.reshape(rows_here, node_count, SUPER),
        precision=lax.Precision.HIGHEST,
        preferred_element_type=jnp.float32,
    )
    diag_inv = diag_block_inv + lax.psum_scatter(partial_diag, "row", scatter_dimension=1, tiled=True)
    return (off_inv, diag_inv)


def solution(mesh):
    rows, cols = mesh.shape["row"], mesh.shape["col"]
    in_specs = (P("row", "col"), P(None, "col"), P("col", "row", None), P())
    out_specs = (P("col", "row"), P("col", "row", None))

    def local(*args):
        return body(rows, cols, *args)

    return jax.shard_map(local, mesh=mesh, in_specs=in_specs, out_specs=out_specs, check_vma=False)
```

time: 592 us -> 563 us (0.951)
  waiting for transfers between devices: 330 us -> 483 us
  blocking collectives: 143 us -> 0 us
  matrix products: 69.6 us -> 45.3 us
  local copies, waits for them, and re-layouts: 21.2 us -> 6.03 us
    all_to_all x1 -> x0, blocking collectives: 143 us -> none  [body(): lax.all_to_all(masked, 'col', split_axis=0, concat_axis=1, tiled=True)]
    all_gather x0 -> x1, waiting for transfers between devices: none -> 133 us  [body(): gathered = lax.all_gather(masked, 'col', axis=1, tiled=True)]
    reduce_scatter x1, waiting for transfers between devices: 256 us -> 153 us  [body(): summed = lax.psum_scatter(partial, 'row', scatter_dimension=0, tiled=True)]
    reduce_scatter x1, waiting for transfers between devices: 74.5 us -> 168 us  [body(): lax.psum_scatter(partial_diag, 'row', scatter_dimension=1, tiled=True)]
    ppermute x0 -> x2, waiting for transfers between devices: none -> 29.4 us  [the longest x1 16.4 us: body(): keep_part = lax.ppermute(keep_part, ('row', 'col'), same)]
    dot_general x1, matrix products: 66 us -> 40.6 us  [body(): lax.dot_general(gathered, ancestor_inv, (((0,), (0,)), ((), ())), precisi...]
    all_to_all x1 -> x0, local copies, waits for them, and re-layouts: 12.6 us -> none  [body(): lax.all_to_all(masked, 'col', split_axis=0, concat_axis=1, tiled=True)]
  transfers between devices with their start and end apart: 2 -> 5, of which waited for: 2 -> 5; matrix products, arithmetic and copies ran while one was open for 1% -> 1% of each run, Pallas kernels for 0% -> 0%
where the time goes in v1:
time: 563 us
  waiting for transfers between devices  483 us (86%)
  matrix products  45.3 us (8%)
  between operations  13.8 us (2%)
  other arithmetic  9.1 us (2%)
  local copies, waits for them, and re-layouts  6.03 us (1%)
    reduce_scatter x1, waiting for transfers between devices, body(): lax.psum_scatter(partial_diag, 'row', scatter_dimension=1, tiled=True)  168 us
    reduce_scatter x1, waiting for transfers between devices, body(): summed = lax.psum_scatter(partial, 'row', scatter_dimension=0, tiled=True)  153 us
    all_gather x1, waiting for transfers between devices, body(): gathered = lax.all_gather(masked, 'col', axis=1, tiled=True)  133 us
    dot_general x1, matrix products, body(): lax.dot_general(gathered, ancestor_inv, (((0,), (0,)), ((), ())), precisi...  40.6 us
    ppermute x1, waiting for transfers between devices, body(): keep_part = lax.ppermute(keep_part, ('row', 'col'), same)  16.4 us
    ppermute x1, waiting for transfers between devices, body(): swap_part = lax.ppermute(swap_part, ('row', 'col'), other)  13 us
  transfers between devices with their start and end apart: 5, of which 5 were waited for; matrix products, arithmetic and copies ran while one was open for 1% of the time, Pallas kernels for 0%

profile of v1, /device:TPU:2, one launch (start us, length us, event | category | flops | bytes accessed | tf_op | source)
XLA Modules:
  0.0 562.6 jit_solution(17553553835792112866)
XLA Ops:
  7.2 0.0 all-gather.2.cloned.1.call-start
  7.2 0.8 dynamic-slice_convert_fusion
  8.0 0.1 copy.11
  8.1 0.5 mul.49
  8.6 2.8 bitcast_multiply_fusion
  11.3 0.0 all-gather.2.cloned.1.call-update
  11.3 0.0 reduce-scatter.3.cloned.1.call-start
  11.4 133.3 %all-gather.2.cloned.1.call-done = f32[1536,4096]{1,0:T(8,128)} async-done(((f32[1536,256]{1,0:T(8,128)}), f32[1536,4096]{1,0:T(8,128)}) %all-gather.2.cloned.1.call-update) | async-done | bytes 25165840 | tf_op jit(solution)/shard_map/all_gather | solution.py:23
  144.7 40.6 %fusion.12 = f32[4096,768]{1,0:T(8,128)} fusion(f32[1536,4096]{1,0:T(8,128)} %all-gather.2.cloned.1.call-done, f32[1536,768]{1,0:T(8,128)} %param.4), kind=kOutput, calls=%fused_computation.22 | convolution fusion | flops 28991029248 | bytes 42467328 | tf_op jit(solution)/shard_map/dot_general | solution.py:24
  185.3 0.0 reduce-scatter.3.cloned.1.call-update
  185.3 0.0 reduce-scatter.5.cloned.1.call-start
  185.4 152.6 %reduce-scatter.3.cloned.1.call-done = f32[512,768]{1,0:T(8,128)} async-done(((f32[4096,768]{1,0:T(8,128)}), f32[512,768]{1,0:T(8,128)}) %reduce-scatter.3.cloned.1.call-update) | async-done | bytes 1572880 | tf_op jit(solution)/shard_map/reduce_scatter | solution.py:31
  338.0 2.6 constant_dynamic-slice_fusion.1
  340.6 3.4 collective-permute-start
  344.0 1.7 collective-permute-start.1
  345.6 1.6 copy.14
  347.2 0.1 broadcast_bitcast_fusion
  347.3 0.8 fusion.15
  348.1 0.1 copy.12
  348.2 0.5 mul.54
  348.7 0.1 copy.23
  348.8 0.5 copy.13
  349.2 16.4 %collective-permute-done = f32[256,768]{1,0:T(8,128)} collective-permute-done((f32[256,768]{1,0:T(8,128)}, f32[256,768]{1,0:T(8,128)}, u32[]{:S(2)}, u32[]{:S(2)}) %collective-permute-start) | collective-permute-done | bytes 786464 | tf_op jit(solution)/shard_map/ppermute | solution.py:40
  365.7 13.0 %collective-permute-done.1 = f32[256,768]{1,0:T(8,128)} collective-permute-done((f32[256,768]{1,0:T(8,128)}, f32[256,768]{1,0:T(8,128)}, u32[]{:S(2)}, u32[]{:S(2)}) %collective-permute-start.1) | collective-permute-done | bytes 786464 | tf_op jit(solution)/shard_map/ppermute | solution.py:41
  378.7 4.7 fusion.2
  383.4 0.0 reduce-scatter.5.cloned.1.call-update
  383.4 0.0 copy-start
  383.4 3.5 fusion.1
  386.9 167.8 %reduce-scatter.5.cloned.1.call-done = f32[2,16,128]{2,1,0:T(8,128)} async-done(((f32[2,128,128]{2,1,0:T(8,128)}), f32[2,16,128]{2,1,0:T(8,128)}) %reduce-scatter.5.cloned.1.call-update) | async-done | bytes 16400 | tf_op jit(solution)/shard_map/reduce_scatter | solution.py:57
  554.7 0.0 copy-done
  554.7 1.3 add.32
  (1 shorter events, 0.0 us)
Async XLA Ops:
  7.2 137.5 %all-gather.2.cloned.1.call-start = ((), (), s32[]{:S(2)}) async-start(), calls=%async_computation.2 | async-start | bytes 26738688 | tf_op jit(solution)/shard_map/all_gather | solution.py:23
  11.3 326.6 %reduce-scatter.3.cloned.1.call-start = ((), (), s32[]{:S(2)}) async-start(), calls=%async_computation.3 | async-start | bytes 14155776 | tf_op jit(solution)/shard_map/reduce_scatter | solution.py:31
  185.3 369.5 %reduce-scatter.5.cloned.1.call-start = ((), (), s32[]{:S(2)}) async-start(), calls=%async_computation.4 | async-start | bytes 147456 | tf_op jit(solution)/shard_map/reduce_scatter | solution.py:57
  340.6 25.1 %collective-permute-start = (f32[256,768]{1,0:T(8,128)}, f32[256,768]{1,0:T(8,128)}, u32[]{:S(2)}, u32[]{:S(2)}) collective-permute-start(f32[256,768]{1,0:T(8,128)} %get-tuple-element.4), channel_id=1, source_target_pairs={{0,0},{1,1},{2,16},{3,17},{4,32},{5,33},{6,48},{7,49},{8,64},{9,65... | collective-permute-start | bytes 2359304 | tf_op jit(solution)/shard_map/ppermute | solution.py:40
  344.0 34.7 %collective-permute-start.1 = (f32[256,768]{1,0:T(8,128)}, f32[256,768]{1,0:T(8,128)}, u32[]{:S(2)}, u32[]{:S(2)}) collective-permute-start(f32[256,768]{1,0:T(8,128)} %get-tuple-element.5), channel_id=1, source_target_pairs={{0,1},{1,0},{2,17},{3,16},{4,33},{5,32},{6,49},{7,48},{8,65},{9,64... | collective-permute-start | bytes 2359304 | tf_op jit(solution)/shard_map/ppermute | solution.py:41
  383.4 171.3 %copy-start = (f32[2,16,128]{2,1,0:T(8,128)S(1)}, f32[2,16,128]{2,1,0:T(8,128)}, u32[]{:S(2)}) copy-start(f32[2,16,128]{2,1,0:T(8,128)} %param.6) | copy-start | bytes 49156
Sparse Core Ops, SparseCore 0:
  11.5 133.1 all-gather.1
  185.4 152.5 reduce-scatter.2
  383.5 171.1 reduce-scatter.4

commit v2 on v0

v2 whole, which is shorter than its diff:
```python
import functools

import jax
import jax.numpy as jnp
from jax import lax
from jax.experimental import pallas as pl
from jax.experimental.pallas import tpu as pltpu
from jax.sharding import PartitionSpec as P

SUPER = 128
MESH = pl.DeviceIdType.MESH
RING = 4
EVENTS = 16


def arrivals():
    table = [[(0, 0, 0, 0), (0, 0, 0, 1)], [(0, 0, 1, 0), (0, 0, 1, 1)]]
    for half in range(2):
        table.append([(0, 1, 0, half), (0, 1, 1, half)])
        for core in range(2):
            table.append([(-1, 0, core, half), (1, 0, core, half)])
    for half in range(2):
        for core in range(2):
            table.append([(-1, 1, core, half), (1, 1, core, half)])
    for dy in range(2):
        for core in range(2):
            table.append([(2, dy, core, 0), (2, dy, core, 1)])
    return table


TABLE = arrivals()
PLACE = {unit: (event, slot) for event, pair in enumerate(TABLE) for slot, unit in enumerate(pair)}


def forwards(unit):
    dx, dy, core, half = unit
    if core:
        return []
    out = []
    if dx == 0:
        if dy == 0:
            out.append(("y", (0, 1, 0, half)))
        out.append(("x+", (-1, dy, 0, half)))
        out.append(("x-", (1, dy, 0, half)))
    if dx == -1 and half == 0:
        out.append(("x+", (2, dy, 0, half)))
    if dx == 1 and half == 1:
        out.append(("x-", (2, dy, 0, half)))
    out.append(("core", (dx, dy, 1, half)))
    return out


SENDS = {}
for _pair in TABLE:
    for _unit in _pair:
        for _way, _name in forwards(_unit):
            SENDS[(_unit, _way)] = len(SENDS)


def split(value):
    high = value.astype(jnp.bfloat16)
    low = (value - high.astype(jnp.float32)).astype(jnp.bfloat16)
    return high, low


def kernel(
    kept, panel, ancestor, diag, off, diag_out,
    gathered, a_high, a_low, m_high, m_low, product, first, second, third, full, home, a_chunk, mine, theirs,
    load_sem, a_sem, gather_send, gather_recv, part_send, part_recv, home_send, home_recv, diag_send, diag_recv,
):
    row, col = lax.axis_index("row"), lax.axis_index("col")
    y_hi, z = row // RING, lax.rem(row, RING)
    x, y_lo, core = col // 4, lax.rem(col // 2, 2), lax.rem(col, 2)
    depth = panel.shape[1]
    width = ancestor.shape[1]
    piece = width // 8
    chip = col // 2

    def col_at(dx, dy, dcore):
        nx = lax.rem(x + (dx + RING), RING)
        ny = 1 - y_lo if dy else y_lo
        nc = 1 - core if dcore else core
        return nx * 4 + ny * 2 + nc

    def row_at(dyh, dz):
        nz = lax.rem(z + (dz + RING), RING)
        return (1 - y_hi if dyh else y_hi) * RING + nz

    ways = {
        "x+": (row, col_at(1, 0, 0)),
        "x-": (row, col_at(-1, 0, 0)),
        "y": (row, col_at(0, 1, 0)),
        "core": (row, col_at(0, 0, 1)),
        "z+": (row_at(0, 1), col),
        "z-": (row_at(0, -1), col),
        "yh": (row_at(1, 0), col),
    }

    def loads():
        return [
            pltpu.make_async_copy(panel.at[half], gathered.at[0, half], load_sem.at[half]) for half in range(2)
        ]

    def a_load(step, slot):
        rows = pl.ds(pl.multiple_of(step * SUPER, SUPER), SUPER)
        return pltpu.make_async_copy(ancestor.at[rows], a_chunk.at[slot], a_sem.at[slot])

    for copy in loads():
        copy.start()
    a_load(0, 0).start()

    barrier = pltpu.get_barrier_semaphore()

    def greet(device):
        pl.semaphore_signal(barrier, inc=1, device_id=device, device_id_type=MESH)

    for device in ways.values():
        greet(device)
    for step in range(1, 8):
        greet((lax.rem(row + step, 8), col))
    home_row = chip

    def greet_sources(step, carry):
        source_row, source_col = step // 2, 2 * row + lax.rem(step, 2)

        @pl.when(jnp.logical_or(source_row != row, source_col != col))
        def _():
            greet((source_row, source_col))

        return carry

    lax.fori_loop(0, 16, greet_sources, 0)
    pl.semaphore_wait(barrier, len(ways) + 7 + 16 - (home_row == row).astype(jnp.int32))

    def gather_copy(unit, way):
        name = dict(forwards(unit))[way]
        event, slot = PLACE[unit]
        to_event, to_slot = PLACE[name]
        return pltpu.make_async_remote_copy(
            src_ref=gathered.at[event, slot],
            dst_ref=gathered.at[to_event, to_slot],
            send_sem=gather_send.at[SENDS[(unit, way)]],
            recv_sem=gather_recv.at[to_event, to_slot],
            device_id=ways[way],
            device_id_type=MESH,
        )

    def arrived(event, slot):
        return pltpu.make_async_remote_copy(
            src_ref=gathered.at[event, slot],
            dst_ref=gathered.at[event, slot],
            send_sem=gather_send.at[0],
            recv_sem=gather_recv.at[event, slot],
            device_id=ways["core"],
            device_id_type=MESH,
        )

    for copy in loads():
        copy.wait()
    for unit in TABLE[0]:
        for way, _ in forwards(unit):
            gather_copy(unit, way).start()

    def convert(step, carry):
        slot = lax.rem(step, 2)

        @pl.when(step + 1 < depth // SUPER)
        def _():
            a_load(step + 1, 1 - slot).start()

        a_load(step, slot).wait()
        high, low = split(a_chunk[slot].T)
        lanes = pl.ds(pl.multiple_of(step * SUPER, SUPER), SUPER)
        a_high[:, lanes] = high
        a_low[:, lanes] = low
        return carry

    lax.fori_loop(0, depth // SUPER, convert, 0)

    def compute(event):
        def prepare(step, carry):
            rows = pl.ds(pl.multiple_of(step * 256, 256), 256)
            for slot in range(2):
                high, low = split(gathered[event, slot, rows, :])
                m_high[rows, slot * SUPER:(slot + 1) * SUPER] = high
                m_low[rows, slot * SUPER:(slot + 1) * SUPER] = low
            return carry

        lax.fori_loop(0, depth // 256, prepare, 0)

        def multiply(step, carry):
            rows = pl.ds(pl.multiple_of(step * (width // 2), width // 2), width // 2)
            high = a_high[rows, :]
            total = jnp.dot(high, m_low[...], preferred_element_type=jnp.float32)
            total += jnp.dot(a_low[rows, :], m_high[...], preferred_element_type=jnp.float32)
            total += jnp.dot(high, m_high[...], preferred_element_type=jnp.float32)
            product[event, rows, :] = total
            return carry

        lax.fori_loop(0, 2, multiply, 0)

    def rows_of(part, dz):
        target = lax.rem(z + (dz + RING), RING) + part * RING
        return pl.ds(pl.multiple_of(target * piece, 8), piece)

    def part_copy(event, index, source, target, recv, way):
        return pltpu.make_async_remote_copy(
            src_ref=source,
            dst_ref=target,
            send_sem=part_send.at[event, index],
            recv_sem=part_recv.at[event, recv],
            device_id=ways[way],
            device_id_type=MESH,
        )

    def copies(event):
        block = product.at[event]
        make = {
            "far_a": lambda: part_copy(event, 0, block.at[rows_of(0, 2)], first.at[event, 0], 0, "z-"),
            "far_b": lambda: part_copy(event, 1, block.at[rows_of(1, 2)], first.at[event, 1], 1, "z+"),
            "near_a": lambda: part_copy(event, 2, block.at[rows_of(0, 1)], second.at[event, 0], 2, "z+"),
            "near_b": lambda: part_copy(event, 3, block.at[rows_of(1, -1)], second.at[event, 1], 3, "z-"),
            "sum_a": lambda: part_copy(event, 4, first.at[event, 0], second.at[event, 2], 4, "z-"),
            "sum_b": lambda: part_copy(event, 5, first.at[event, 1], second.at[event, 3], 5, "z+"),
            "yh": lambda: part_copy(
                event, 6,
                block.at[pl.ds(pl.multiple_of(((1 - y_hi) * RING + z) * piece, 8), piece)],
                third.at[event], 6, "yh",
            ),
        }
        return make

    def stage_send(event):
        table = copies(event)
        for name in ("far_a", "far_b", "near_a", "near_b"):
            table[name]().start()

    def stage_pass(event):
        table = copies(event)
        table["far_a"]().wait_recv()
        first[event, 0] = first[event, 0] + product[event, rows_of(0, -1), :]
        table["sum_a"]().start()
        table["far_b"]().wait_recv()
        first[event, 1] = first[event, 1] + product[event, rows_of(1, 1), :]
        table["sum_b"]().start()

    def stage_cross(event):
        table = copies(event)
        for name in ("near_a", "near_b", "sum_a", "sum_b"):
            table[name]().wait_recv()
        for part in range(2):
            rows = rows_of(part, 0)
            product[event, rows, :] = product[event, rows, :] + second[event, part] + second[event, part + 2]
        table["yh"]().start()

    home_rows = pl.ds(pl.multiple_of(lax.rem(col, 2) * width + row * piece, 8), piece)

    def home_copy(event, slot):
        dx, dy, dcore, half = TABLE[event][slot]
        target = col_at(dx, dy, dcore)
        recv = home_recv.at[lax.rem(col, 2) * 16 + row * 2 + half]
        return pltpu.make_async_remote_copy(
            src_ref=full.at[event, slot],
            dst_ref=home.at[half, home_rows],
            send_sem=home_send.at[event, slot],
            recv_sem=recv,
            device_id=(home_row, target),
            device_id_type=MESH,
        )

    def stays(event, slot):
        half = TABLE[event][slot][3]
        return pltpu.make_async_copy(
            full.at[event, slot],
            home.at[half, home_rows],
            home_recv.at[lax.rem(col, 2) * 16 + row * 2 + half],
        )

    def stage_home(event):
        copies(event)["yh"]().wait_recv()
        total = product[event, pl.ds(pl.multiple_of(row * piece, 8), piece), :] + third[event]
        for slot in range(2):
            full[event, slot] = total[:, slot * SUPER:(slot + 1) * SUPER]
            if TABLE[event][slot][:3] == (0, 0, 0):

                @pl.when(home_row != row)
                def _():
                    home_copy(event, slot).start()

                @pl.when(home_row == row)
                def _():
                    stays(event, slot).start()
            else:
                home_copy(event, slot).start()

    for event in range(EVENTS + 3):
        if event < EVENTS:
            for slot, unit in enumerate(TABLE[event]):
                if event > 0:
                    arrived(event, slot).wait_recv()
                    for way, _ in forwards(unit):
                        gather_copy(unit, way).start()
            compute(event)
            stage_send(event)
        if 0 <= event - 1 < EVENTS:
            stage_pass(event - 1)
        if 0 <= event - 2 < EVENTS:
            stage_cross(event - 2)
        if 0 <= event - 3 < EVENTS:
            stage_home(event - 3)

    def home_wait(step, carry):
        side, source, half = step // 16, lax.rem(step // 2, 8), lax.rem(step, 2)
        rows = pl.ds(pl.multiple_of(side * width + source * piece, 8), piece)
        pltpu.make_async_copy(home.at[half, rows], home.at[half, rows], home_recv.at[step]).wait()
        return carry

    lax.fori_loop(0, 32, home_wait, 0)

    blocks = depth // SUPER
    for half in range(2):
        total = jnp.zeros((SUPER, SUPER), jnp.float32)
        for block in range(blocks):
            rows = slice(block * SUPER, (block + 1) * SUPER)
            tile = home[half, rows, :].T
            off[half * SUPER:(half + 1) * SUPER, rows] = tile * (-kept[block, half])
            t_high, t_low = split(tile)
            p_high, p_low = split(gathered[0, half, rows, :])
            total += jnp.dot(t_high, p_low, preferred_element_type=jnp.float32)
            total += jnp.dot(t_low, p_high, preferred_element_type=jnp.float32)
            total += jnp.dot(t_high, p_high, preferred_element_type=jnp.float32)
        share = SUPER // 8
        for target in range(8):
            mine[target, half] = total[target * share:(target + 1) * share]

    def diag_copy(step):
        target = lax.rem(row + step, 8)
        return pltpu.make_async_remote_copy(
            src_ref=mine.at[target],
            dst_ref=theirs.at[step],
            send_sem=diag_send.at[step],
            recv_sem=diag_recv.at[step],
            device_id=(target, col),
            device_id_type=MESH,
        )

    for step in range(1, 8):
        diag_copy(step).start()
    total = diag[...] + mine[row]
    for step in range(1, 8):
        diag_copy(step).wait_recv()
        total += theirs[step]
    diag_out[...] = total

    for step in range(1, 8):
        diag_copy(step).wait_send()
    for (unit, way) in SENDS:
        gather_copy(unit, way).wait_send()
    for event in range(EVENTS):
        for make in copies(event).values():
            make().wait_send()
        for slot in range(2):
            if TABLE[event][slot][:3] == (0, 0, 0):

                @pl.when(home_row != row)
                def _():
                    home_copy(event, slot).wait_send()
            else:
                home_copy(event, slot).wait_send()


def body(ancestor_inv, lower_panel, diag_block_inv, pattern):
    depth, width = ancestor_inv.shape
    width_here = lower_panel.shape[1]
    node_count = width_here // SUPER
    row_blocks = depth // SUPER
    col_index = lax.axis_index("col")
    row_index = lax.axis_index("row")
    kept = lax.dynamic_slice(
        pattern, (row_index * row_blocks, col_index * node_count), (row_blocks, node_count)
    ).astype(jnp.float32)
    panel_rows = lax.dynamic_slice_in_dim(lower_panel, row_index * depth, depth, 0)
    masked = panel_rows.reshape(row_blocks, SUPER, node_count, SUPER) * kept[:, None, :, None]
    units = jnp.transpose(masked.reshape(depth, node_count, SUPER), (1, 0, 2))
    piece = width // 8
    share = SUPER // 8
    f32, bf16 = jnp.float32, jnp.bfloat16
    off, diag = pl.pallas_call(
        kernel,
        out_shape=(
            jax.ShapeDtypeStruct((width_here, depth), f32),
            jax.ShapeDtypeStruct(diag_block_inv.shape, f32),
        ),
        in_specs=[
            pl.BlockSpec(memory_space=pltpu.SMEM),
            pl.BlockSpec(memory_space=pl.ANY),
            pl.BlockSpec(memory_space=pl.ANY),
            pl.BlockSpec(memory_space=pltpu.VMEM),
        ],
        out_specs=(pl.BlockSpec(memory_space=pltpu.VMEM), pl.BlockSpec(memory_space=pltpu.VMEM)),
        scratch_shapes=[
            pltpu.VMEM((EVENTS, 2, depth, SUPER), f32),
            pltpu.VMEM((width, depth), bf16),
            pltpu.VMEM((width, depth), bf16),
            pltpu.VMEM((depth, 2 * SUPER), bf16),
            pltpu.VMEM((depth, 2 * SUPER), bf16),
            pltpu.VMEM((EVENTS, width, 2 * SUPER), f32),
            pltpu.VMEM((EVENTS, 2, piece, 2 * SUPER), f32),
            pltpu.VMEM((EVENTS, 4, piece, 2 * SUPER), f32),
            pltpu.VMEM((EVENTS, piece, 2 * SUPER), f32),
            pltpu.VMEM((EVENTS, 2, piece, SUPER), f32),
            pltpu.VMEM((2, depth, SUPER), f32),
            pltpu.VMEM((2, SUPER, width), f32),
            pltpu.VMEM((8, 2, share, SUPER), f32),
            pltpu.VMEM((8, 2, share, SUPER), f32),
            pltpu.SemaphoreType.DMA((2,)),
            pltpu.SemaphoreType.DMA((2,)),
            pltpu.SemaphoreType.DMA((len(SENDS),)),
            pltpu.SemaphoreType.DMA((EVENTS, 2)),
            pltpu.SemaphoreType.DMA((EVENTS, 7)),
            pltpu.SemaphoreType.DMA((EVENTS, 7)),
            pltpu.SemaphoreType.DMA((EVENTS, 2)),
            pltpu.SemaphoreType.DMA((32,)),
            pltpu.SemaphoreType.DMA((8,)),
            pltpu.SemaphoreType.DMA((8,)),
        ],
        compiler_params=pltpu.CompilerParams(
            collective_id=0, has_side_effects=True, vmem_limit_bytes=63 * 2**20
        ),
        cost_estimate=pl.CostEstimate(
            flops=6 * depth * width * 16 * 2 * SUPER, bytes_accessed=16 * 2**20, transcendentals=0
        ),
    )(kept, units, ancestor_inv, diag_block_inv)
    return (off, diag)


def solution(mesh):
    in_specs = (P("row", "col"), P(None, "col"), P("col", "row", None), P())
    out_specs = (P("col", "row"), P("col", "row", None))
    return jax.shard_map(body, mesh=mesh, in_specs=in_specs, out_specs=out_specs, check_vma=False)
```

time: 592 us -> 208 us (0.35)
  waiting for transfers between devices: 330 us -> 0 us
  Pallas kernels: 0 us -> 198 us
  blocking collectives: 143 us -> 0 us
  matrix products: 69.6 us -> 0 us
  local copies, waits for them, and re-layouts: 21.2 us -> 6.75 us
  between operations: 14.1 us -> 0.69 us
  other arithmetic: 12.9 us -> 1.63 us
    reduce_scatter x2 -> x0, waiting for transfers between devices: 330 us -> none  [the longest x1 256 us: body(): lax.psum_scatter(lax.dot_general(relaid, ancestor_inv, (((0,), (1,)), (()...]
    pallas_call x0 -> x1, Pallas kernels: none -> 198 us  [body(): pl.pallas_call(kernel, out_shape=(jax.ShapeDtypeStruct((width_here, depth...]
    all_to_all x1 -> x0, blocking collectives: 143 us -> none  [body(): lax.all_to_all(masked, 'col', split_axis=0, concat_axis=1, tiled=True)]
    dot_general x2 -> x0, matrix products: 69.6 us -> none  [the longest x1 66 us: body(): lax.dot_general(relaid, ancestor_inv, (((0,), (1,)), ((), ())), precision...]
    all_to_all x1 -> x0, local copies, waits for them, and re-layouts: 12.6 us -> none  [body(): lax.all_to_all(masked, 'col', split_axis=0, concat_axis=1, tiled=True)]
    mul x1 -> x0, other arithmetic: 7.58 us -> none  [body(): lower_panel.reshape(block_count, SUPER, node_count, SUPER)]
    mul x3 -> x0, local copies, waits for them, and re-layouts: 6.26 us -> none  [the longest x1 4.17 us: body(): lower_panel.reshape(block_count, SUPER, node_count, SUPER)]
  transfers between devices with their start and end apart: 2 -> 0, of which waited for: 2 -> 0; matrix products, arithmetic and copies ran while one was open for 1% -> 0% of each run, Pallas kernels for 0% -> 0%
where the time goes in v2:
time: 208 us; the launch traced here: 207 us
  Pallas kernels  198 us (95%)
  local copies, waits for them, and re-layouts  6.75 us (3%)
    pallas_call x1, Pallas kernels, body(): pl.pallas_call(kernel, out_shape=(jax.ShapeDtypeStruct((width_here, depth...  198 us

profile of v2, /device:TPU:2, one launch (start us, length us, event | category | flops | bytes accessed | tf_op | source)
XLA Modules:
  0.0 207.4 jit_solution(17166638171620796913)
XLA Ops:
  0.6 0.8 dynamic_slice.6
  1.4 0.1 copy.12
  1.5 0.0 copy-start
  1.5 0.1 copy.10
  1.6 0.1 broadcast_bitcast_fusion
  1.7 1.5 constant_dynamic-slice_fusion
  3.2 0.0 copy-done
  3.2 0.5 copy.13
  3.7 0.5 copy.11
  4.2 1.6 multiply_bitcast_fusion.panel
  5.8 198.4 %shard_map.59 = (f32[256,1536]{1,0:T(8,128)}, f32[2,16,128]{2,1,0:T(8,128)}) custom-call(f32[12,2]{1,0:T(8,128)} %copy-done, f32[2,1536,128]{2,1,0:T(8,128)} %multiply_bitcast_fusion.panel, f32[1536,768]{1,0:T(8,128)} %ancestor.1, f32[2,16,128]{2,1,0:T(8,128)} %diag.1), custom_call_target="tpu_custom_call" | custom-call | flops 28991029248 | bytes 16777216 | tf_op jit(solution)/shard_map/pallas_call | solution.py:388
  204.1 0.0 copy-start.1
  204.1 2.7 %copy.19 = f32[256,1536]{1,0:T(8,128)} copy(f32[256,1536]{1,0:T(8,128)} %get-tuple-element.4) | data formatting | bytes 3145728
  206.8 0.0 copy-done.1
  206.8 0.6 copy.20
  (2 shorter events, 0.0 us)
Async XLA Ops:
  1.5 1.7 copy-start
  204.1 2.7 %copy-start.1 = (f32[2,16,128]{2,1,0:T(8,128)S(1)}, f32[2,16,128]{2,1,0:T(8,128)}, u32[]{:S(2)}) copy-start(f32[2,16,128]{2,1,0:T(8,128)} %get-tuple-element.5) | copy-start | bytes 49156

commit v3 on v2

--- a/solution.py
+++ b/solution.py
@@ -64,17 +64,17 @@
 
 
 def kernel(
-    kept, panel, ancestor, diag, off, diag_out,
-    gathered, a_high, a_low, m_high, m_low, product, first, second, third, full, home, a_chunk, mine, theirs,
-    load_sem, a_sem, gather_send, gather_recv, part_send, part_recv, home_send, home_recv, diag_send, diag_recv,
+    pattern, panel, ancestor, diag, off, diag_out,
+    gathered, a_high, a_low, m_high, m_low, product, first, second, third, full, relay, home, a_chunk, mine, theirs,
+    load_sem, a_sem, gather_send, gather_recv, part_send, part_recv, relay_send, relay_recv, home_send, home_recv,
+    diag_send, diag_recv,
 ):
     row, col = lax.axis_index("row"), lax.axis_index("col")
     y_hi, z = row // RING, lax.rem(row, RING)
     x, y_lo, core = col // 4, lax.rem(col // 2, 2), lax.rem(col, 2)
-    depth = panel.shape[1]
-    width = ancestor.shape[1]
+    depth, width = ancestor.shape
+    blocks = depth // SUPER
     piece = width // 8
-    chip = col // 2
 
     def col_at(dx, dy, dcore):
         nx = lax.rem(x + (dx + RING), RING)
@@ -97,9 +97,16 @@
     }
 
     def loads():
+        rows = pl.ds(pl.multiple_of(row * depth, SUPER), depth)
         return [
-            pltpu.make_async_copy(panel.at[half], gathered.at[0, half], load_sem.at[half]) for half in range(2)
+            pltpu.make_async_copy(
+                panel.at[rows, pl.ds(half * SUPER, SUPER)], gathered.at[0, half], load_sem.at[half]
+            )
+            for half in range(2)
         ]
+
+    def kept(block, half):
+        return pattern[row * blocks + block, col * 2 + half].astype(jnp.float32)
 
     def a_load(step, slot):
         rows = pl.ds(pl.multiple_of(step * SUPER, SUPER), SUPER)
@@ -116,21 +123,7 @@
 
     for device in ways.values():
         greet(device)
-    for step in range(1, 8):
-        greet((lax.rem(row + step, 8), col))
-    home_row = chip
-
-    def greet_sources(step, carry):
-        source_row, source_col = step // 2, 2 * row + lax.rem(step, 2)
-
-        @pl.when(jnp.logical_or(source_row != row, source_col != col))
-        def _():
-            greet((source_row, source_col))
-
-        return carry
-
-    lax.fori_loop(0, 16, greet_sources, 0)
-    pl.semaphore_wait(barrier, len(ways) + 7 + 16 - (home_row == row).astype(jnp.int32))
+    pl.semaphore_wait(barrier, len(ways))
 
     def gather_copy(unit, way):
         name = dict(forwards(unit))[way]
@@ -155,9 +148,15 @@
             device_id_type=MESH,
         )
 
-    for copy in loads():
-        copy.wait()
-    for unit in TABLE[0]:
+    for half, unit in enumerate(TABLE[0]):
+        loads()[half].wait()
+
+        def mask(block, carry):
+            rows = pl.ds(pl.multiple_of(block * SUPER, SUPER), SUPER)
+            gathered[0, half, rows, :] = gathered[0, half, rows, :] * kept(block, half)
+            return carry
+
+        lax.fori_loop(0, blocks, mask, 0)
         for way, _ in forwards(unit):
             gather_copy(unit, way).start()
 
@@ -253,47 +252,62 @@
             product[event, rows, :] = product[event, rows, :] + second[event, part] + second[event, part + 2]
         table["yh"]().start()
 
-    home_rows = pl.ds(pl.multiple_of(lax.rem(col, 2) * width + row * piece, 8), piece)
-
-    def home_copy(event, slot):
-        dx, dy, dcore, half = TABLE[event][slot]
-        target = col_at(dx, dy, dcore)
-        recv = home_recv.at[lax.rem(col, 2) * 16 + row * 2 + half]
+    def relay_copy(event, slot):
+        dx, dy, dcore, _ = TABLE[event][slot]
         return pltpu.make_async_remote_copy(
             src_ref=full.at[event, slot],
-            dst_ref=home.at[half, home_rows],
-            send_sem=home_send.at[event, slot],
-            recv_sem=recv,
-            device_id=(home_row, target),
+            dst_ref=relay.at[event, slot],
+            send_sem=relay_send.at[event, slot],
+            recv_sem=relay_recv.at[event, slot],
+            device_id=(row, col_at(dx, dy, dcore)),
             device_id_type=MESH,
         )
 
-    def stays(event, slot):
-        half = TABLE[event][slot][3]
-        return pltpu.make_async_copy(
-            full.at[event, slot],
-            home.at[half, home_rows],
-            home_recv.at[lax.rem(col, 2) * 16 + row * 2 + half],
-        )
-
-    def stage_home(event):
+    def home_step(event, slot, wait_only=False):
+        dx, dy, dcore, half = TABLE[event][slot]
+        source_col = col_at(-dx, dy, dcore)
+        target_row = source_col // 2
+        rows = pl.ds(pl.multiple_of(lax.rem(source_col, 2) * width + row * piece, 8), piece)
+        source = (full if (dx, dy, dcore) == (0, 0, 0) else relay).at[event, slot]
+        recv = home_recv.at[lax.rem(source_col, 2) * 16 + row * 2 + half]
+        remote = target_row != row
+
+        @pl.when(remote)
+        def _():
+            copy = pltpu.make_async_remote_copy(
+                src_ref=source,
+                dst_ref=home.at[half, rows],
+                send_sem=home_send.at[event, slot],
+                recv_sem=recv,
+                device_id=(target_row, col),
+                device_id_type=MESH,
+            )
+            if wait_only:
+                copy.wait_send()
+            else:
+                copy.start()
+
+        if not wait_only:
+
+            @pl.when(jnp.logical_not(remote))
+            def _():
+                pltpu.make_async_copy(source, home.at[half, rows], recv).start()
+
+    def stage_relay(event):
         copies(event)["yh"]().wait_recv()
         total = product[event, pl.ds(pl.multiple_of(row * piece, 8), piece), :] + third[event]
         for slot in range(2):
             full[event, slot] = total[:, slot * SUPER:(slot + 1) * SUPER]
-            if TABLE[event][slot][:3] == (0, 0, 0):
-
-                @pl.when(home_row != row)
-                def _():
-                    home_copy(event, slot).start()
-
-                @pl.when(home_row == row)
-                def _():
-                    stays(event, slot).start()
-            else:
-                home_copy(event, slot).start()
-
-    for event in range(EVENTS + 3):
+            if TABLE[event][slot][:3] != (0, 0, 0):
+                relay_copy(event, slot).start()
+
+    def stage_home(event):
+        for slot in range(2):
+            if TABLE[event][slot][:3] != (0, 0, 0):
+                relay_copy(event, slot).wait_recv()
+            home_step(event, slot)
+
+    for event in range(EVENTS + 4):
         if event < EVENTS:
             for slot, unit in enumerate(TABLE[event]):
                 if event > 0:
@@ -307,7 +321,9 @@
         if 0 <= event - 2 < EVENTS:
             stage_cross(event - 2)
         if 0 <= event - 3 < EVENTS:
-            stage_home(event - 3)
+            stage_relay(event - 3)
+        if 0 <= event - 4 < EVENTS:
+            stage_home(event - 4)
 
     def home_wait(step, carry):
         side, source, half = step // 16, lax.rem(step // 2, 8), lax.rem(step, 2)
@@ -317,13 +333,12 @@
 
     lax.fori_loop(0, 32, home_wait, 0)
 
-    blocks = depth // SUPER
     for half in range(2):
         total = jnp.zeros((SUPER, SUPER), jnp.float32)
         for block in range(blocks):
             rows = slice(block * SUPER, (block + 1) * SUPER)
             tile = home[half, rows, :].T
-            off[half * SUPER:(half + 1) * SUPER, rows] = tile * (-kept[block, half])
+            off[half * SUPER:(half + 1) * SUPER, rows] = tile * (-kept(block, half))
             t_high, t_low = split(tile)
             p_high, p_low = split(gathered[0, half, rows, :])
             total += jnp.dot(t_high, p_low, preferred_element_type=jnp.float32)
@@ -360,28 +375,14 @@
         for make in copies(event).values():
             make().wait_send()
         for slot in range(2):
-            if TABLE[event][slot][:3] == (0, 0, 0):
-
-                @pl.when(home_row != row)
-                def _():
-                    home_copy(event, slot).wait_send()
-            else:
-                home_copy(event, slot).wait_send()
+            if TABLE[event][slot][:3] != (0, 0, 0):
+                relay_copy(event, slot).wait_send()
+            home_step(event, slot, wait_only=True)
 
 
 def body(ancestor_inv, lower_panel, diag_block_inv, pattern):
     depth, width = ancestor_inv.shape
     width_here = lower_panel.shape[1]
-    node_count = width_here // SUPER
-    row_blocks = depth // SUPER
-    col_index = lax.axis_index("col")
-    row_index = lax.axis_index("row")
-    kept = lax.dynamic_slice(
-        pattern, (row_index * row_blocks, col_index * node_count), (row_blocks, node_count)
-    ).astype(jnp.float32)
-    panel_rows = lax.dynamic_slice_in_dim(lower_panel, row_index * depth, depth, 0)
-    masked = panel_rows.reshape(row_blocks, SUPER, node_count, SUPER) * kept[:, None, :, None]
-    units = jnp.transpose(masked.reshape(depth, node_count, SUPER), (1, 0, 2))
     piece = width // 8
     share = SUPER // 8
     f32, bf16 = jnp.float32, jnp.bfloat16
@@ -409,6 +410,7 @@
             pltpu.VMEM((EVENTS, 4, piece, 2 * SUPER), f32),
             pltpu.VMEM((EVENTS, piece, 2 * SUPER), f32),
             pltpu.VMEM((EVENTS, 2, piece, SUPER), f32),
+            pltpu.VMEM((EVENTS, 2, piece, SUPER), f32),
             pltpu.VMEM((2, depth, SUPER), f32),
             pltpu.VMEM((2, SUPER, width), f32),
             pltpu.VMEM((8, 2, share, SUPER), f32),
@@ -420,6 +422,8 @@
             pltpu.SemaphoreType.DMA((EVENTS, 7)),
             pltpu.SemaphoreType.DMA((EVENTS, 7)),
             pltpu.SemaphoreType.DMA((EVENTS, 2)),
+            pltpu.SemaphoreType.DMA((EVENTS, 2)),
+            pltpu.SemaphoreType.DMA((EVENTS, 2)),
             pltpu.SemaphoreType.DMA((32,)),
             pltpu.SemaphoreType.DMA((8,)),
             pltpu.SemaphoreType.DMA((8,)),
@@ -430,7 +434,7 @@
         cost_estimate=pl.CostEstimate(
             flops=6 * depth * width * 16 * 2 * SUPER, bytes_accessed=16 * 2**20, transcendentals=0
         ),
-    )(kept, units, ancestor_inv, diag_block_inv)
+    )(pattern, lower_panel, ancestor_inv, diag_block_inv)
     return (off, diag)
 
 

time: 208 us -> 219 us (1.053)
  Pallas kernels: 198 us -> 212 us
    pallas_call x1, Pallas kernels: 198 us -> 212 us  [body(): pl.pallas_call(kernel, out_shape=(jax.ShapeDtypeStruct((width_here, depth...]
    dynamic_slice x2 -> x0, local copies, waits for them, and re-layouts: 2.28 us -> none  [the longest x1 1.51 us: body(): lax.dynamic_slice_in_dim(lower_panel, row_index * depth, depth, 0)]
    unnamed x10 -> x3, local copies, waits for them, and re-layouts: 3.92 us -> 5.41 us
where the time goes in v3:
time: 219 us; the launch traced here: 218 us
  Pallas kernels  212 us (97%)
  local copies, waits for them, and re-layouts  5.41 us (2%)
    pallas_call x1, Pallas kernels, body(): pl.pallas_call(kernel, out_shape=(jax.ShapeDtypeStruct((width_here, depth...  212 us
    unnamed x3, local copies, waits for them, and re-layouts  5.41 us

profile of v3, /device:TPU:2, one launch (start us, length us, event | category | flops | bytes accessed | tf_op | source)
XLA Modules:
  0.0 218.1 jit_solution(15345422963659145228)
XLA Ops:
  0.6 1.4 copy.6.pattern
  2.1 212.0 %shard_map.59 = (f32[256,1536]{1,0:T(8,128)}, f32[2,16,128]{2,1,0:T(8,128)}) custom-call(s32[96,32]{1,0:T(8,128)} %copy.6.pattern, f32[12288,256]{1,0:T(8,128)} %panel.1, f32[1536,768]{1,0:T(8,128)} %ancestor.1, f32[2,16,128]{2,1,0:T(8,128)} %diag.1), custom_call_target="tpu_custom_call" | custom-call | flops 28991029248 | bytes 16777216 | tf_op jit(solution)/shard_map/pallas_call | solution.py:389
  214.1 2.7 %copy.9 = f32[256,1536]{1,0:T(8,128)} copy(f32[256,1536]{1,0:T(8,128)} %get-tuple-element.4) | data formatting | bytes 3145728
  216.8 1.3 copy.10

commit v4 on v0

v4 whole, which is shorter than its diff:
```python
import jax
import jax.numpy as jnp
from jax import lax
from jax.experimental import pallas as pl
from jax.experimental.pallas import tpu as pltpu
from jax.sharding import PartitionSpec as P

SUPER = 128
MESH = pl.DeviceIdType.MESH
RING = 4
ROWS = 8
SHARE = 32

SOURCES = ((0, 0), (0, 1), (-1, 0), (1, 0), (-1, 1), (1, 1), (2, 0), (2, 1))
HEAD = tuple((dx, dy, place) for dx, place in ((2, (0, 0)), (1, (1, 0)), (-1, (0, 1)), (0, (1, 1))) for dy in range(2))


def forwards(source, half):
    dz, dy = SOURCES[source]
    out = []
    if dz == 0:
        if dy == 0:
            out.append(("yh", SOURCES.index((0, 1))))
        out.append(("z+", SOURCES.index((-1, dy))))
        out.append(("z-", SOURCES.index((1, dy))))
    if dz == -1 and half == 0:
        out.append(("z+", SOURCES.index((2, dy))))
    if dz == 1 and half == 1:
        out.append(("z-", SOURCES.index((2, dy))))
    out.append(("core", source))
    return out


SENDS = {}
for _source in range(ROWS):
    for _half in range(2):
        for _way, _ in forwards(_source, _half):
            SENDS[(_source, _half, _way)] = len(SENDS)

ORDER = (
    ("arrive", 0, 0),
    ("arrive", 0, 1),
    ("product", 0, 0),
    ("product", 0, 1),
    ("minus", 0),
    ("plus", 0),
    ("arrive", 2, 0),
    ("arrive", 3, 0),
    ("arrive", 1, 0),
    ("own", 0),
    ("product", 2, 0),
    ("product", 3, 0),
    ("product", 1, 0),
    ("minus", 2),
    ("pair", 0),
    ("arrive", 2, 1),
    ("arrive", 3, 1),
    ("arrive", 1, 1),
    ("product", 2, 1),
    ("minus", 3),
    ("plus", 2),
    ("product", 3, 1),
    ("plus", 3),
    ("product", 1, 1),
    ("minus", 1),
    ("plus", 1),
    ("arrive", 5, 0),
    ("arrive", 6, 0),
    ("product", 5, 0),
    ("product", 6, 0),
    ("own", 2),
    ("own", 3),
    ("arrive", 4, 0),
    ("arrive", 6, 1),
    ("pair", 2),
    ("minus", 5),
    ("own", 1),
    ("pair", 3),
    ("product", 4, 0),
    ("product", 6, 1),
    ("minus", 6),
    ("plus", 6),
    ("pair", 1),
    ("arrive", 4, 1),
    ("arrive", 5, 1),
    ("product", 4, 1),
    ("minus", 4),
    ("plus", 4),
    ("product", 5, 1),
    ("plus", 5),
    ("own", 6),
    ("arrive", 7, 0),
    ("own", 4),
    ("arrive", 7, 1),
    ("pair", 6),
    ("product", 7, 0),
    ("product", 7, 1),
    ("own", 5),
    ("pair", 4),
    ("minus", 7),
    ("plus", 7),
    ("pair", 5),
    ("own", 7),
    ("pair", 7),
)


def split(value):
    high = value.astype(jnp.bfloat16)
    low = (value - high.astype(jnp.float32)).astype(jnp.bfloat16)
    return high, low


def kernel(
    pattern, panel, ancestor, diag, off, diag_out,
    gathered, a_high, a_low, m_high, m_low, product, far, near, crossed, result, chunk, turned, pieces, mine, theirs,
    chunk_sem, a_sem, a_send, a_recv, head_send, head_recv, gather_send, gather_recv, part_send, part_recv,
    core_send, core_recv, diag_send, diag_recv,
):
    row, col = lax.axis_index("row"), lax.axis_index("col")
    y_hi, z = row // RING, lax.rem(row, RING)
    x, y_lo, core = col // 4, lax.rem(col // 2, 2), lax.rem(col, 2)
    rows_here, cols_here = ancestor.shape
    depth = rows_here
    blocks = depth // SUPER
    half_rows = rows_here // 2

    def col_at(dx, dy, target_core):
        nx = lax.rem(x + (dx + RING), RING)
        ny = 1 - y_lo if dy else y_lo
        return nx * 4 + ny * 2 + target_core

    def row_at(dz, dy):
        nz = lax.rem(z + (dz + RING), RING)
        return (1 - y_hi if dy else y_hi) * RING + nz

    ways = {
        "x+": (row, col_at(1, 0, core)),
        "x-": (row, col_at(-1, 0, core)),
        "y": (row, col_at(0, 1, core)),
        "core": (row, col_at(0, 0, 1 - core)),
        "z+": (row_at(1, 0), col),
        "z-": (row_at(-1, 0), col),
        "yh": (row_at(0, 1), col),
    }

    def remote(source, target, send, recv, device):
        return pltpu.make_async_remote_copy(
            src_ref=source, dst_ref=target, send_sem=send, recv_sem=recv, device_id=device, device_id_type=MESH
        )

    barrier = pltpu.get_barrier_semaphore()

    def greet(device):
        pl.semaphore_signal(barrier, inc=1, device_id=device, device_id_type=MESH)

    def greet_row(step, carry):
        greet((row, lax.rem(col + step, 16)))
        return carry

    lax.fori_loop(1, 16, greet_row, 0)
    for way in ("z+", "z-", "yh"):
        greet(ways[way])

    def chunk_load(message):
        dx, dy, _ = HEAD[message]
        chip = col_at(dx, dy, 0) // 2
        rows = pl.ds(pl.multiple_of(chip * depth, SUPER), depth)
        lanes = pl.ds(pl.multiple_of((row // 4) * SUPER, SUPER), SUPER)
        return pltpu.make_async_copy(panel.at[rows, lanes], chunk.at[message % 2], chunk_sem.at[message % 2])

    def a_rows(which, part):
        return ancestor.at[pl.ds(pl.multiple_of(which * half_rows + part * 256, 256), 256)]

    own_place = ((2, 0), (2, 1), (3, 0))
    other_place = ((3, 1), (4, 0), (4, 1))

    def a_load(part):
        slot, half = own_place[part]
        return pltpu.make_async_copy(a_rows(core, part), product.at[slot, half], a_sem.at[part])

    def a_swap(part):
        slot, half = other_place[part]
        return remote(
            a_rows(1 - core, part), product.at[slot, half], a_send.at[part], a_recv.at[part], ways["core"]
        )

    chunk_load(0).start()
    chunk_load(1).start()
    for part in range(3):
        a_load(part).start()

    def kept(block_row, column):
        return pattern[block_row, column].astype(jnp.float32)

    def head_copy(message):
        dx, dy, (target_core, half) = HEAD[message]
        piece = y_lo * 2 + core
        return remote(
            pieces.at[message],
            gathered.at[0, target_core, half, pl.ds(pl.multiple_of(piece * SHARE, SHARE), SHARE)],
            head_send.at[message],
            head_recv.at[half, piece],
            (row, col_at(dx, dy, target_core)),
        )

    def head_stay(message):
        _, _, (target_core, half) = HEAD[message]
        piece = y_lo * 2 + core
        return pltpu.make_async_copy(
            pieces.at[message],
            gathered.at[0, target_core, half, pl.ds(pl.multiple_of(piece * SHARE, SHARE), SHARE)],
            head_recv.at[half, piece],
        )

    def stays(message):
        dx, dy, (target_core, _) = HEAD[message]
        return core == target_core if (dx, dy) == (0, 0) else None

    def turn(message):
        dx, dy, _ = HEAD[message]
        chip = col_at(dx, dy, 0) // 2
        chunk_load(message).wait()

        def block_turn(block, carry):
            rows = pl.ds(pl.multiple_of(block * SUPER, SUPER), SUPER)
            tile = chunk[message % 2, rows, :] * kept(chip * blocks + block, col * 2 + row // 4)
            turned[:, rows] = tile.T
            return carry

        lax.fori_loop(0, blocks, block_turn, 0, unroll=2)
        if message + 2 < len(HEAD):
            chunk_load(message + 2).start()
        pieces[message] = turned[pl.ds(pl.multiple_of(lax.rem(row, 4) * SHARE, SHARE), SHARE), :]

    turn(0)
    pl.semaphore_wait(barrier, 18)
    for part in range(3):
        a_swap(part).start()
    for message in range(len(HEAD)):
        if message > 0:
            turn(message)
        if stays(message) is None:
            head_copy(message).start()
        else:

            @pl.when(stays(message))
            def _():
                head_stay(message).start()

            @pl.when(jnp.logical_not(stays(message)))
            def _():
                head_copy(message).start()

    def convert(place, part, offset):
        slot, half = place[part]
        for step in range(2):
            for side in range(cols_here // 256):
                tile = product[slot, half, step * SUPER:(step + 1) * SUPER, side * 256:(side + 1) * 256].T
                high, low = split(tile)
                rows = pl.ds(pl.multiple_of(offset + side * 256, 256), 256)
                lanes = slice(part * 256 + step * SUPER, part * 256 + (step + 1) * SUPER)
                a_high[rows, lanes] = high
                a_low[rows, lanes] = low

    for part in range(3):
        a_load(part).wait()
        convert(own_place, part, core * cols_here)
    for part in range(3):
        a_swap(part).wait_recv()
        convert(other_place, part, (1 - core) * cols_here)

    def gather_copy(source, half, way):
        target = dict(forwards(source, half))[way]
        return remote(
            gathered.at[source, core, half],
            gathered.at[target, core, half],
            gather_send.at[SENDS[(source, half, way)]],
            gather_recv.at[target, core, half],
            ways[way],
        )

    def landed(source, which, half):
        place = gathered.at[source, which, half]
        pltpu.make_async_copy(place, place, gather_recv.at[source, which, half]).wait()

    def arrive(source, half):
        if source == 0:
            for piece in range(4):
                place = gathered.at[0, core, half, pl.ds(piece * SHARE, SHARE)]
                pltpu.make_async_copy(place, place, head_recv.at[half, piece]).wait()
        else:
            landed(source, core, half)
        for way, _ in forwards(source, half):
            gather_copy(source, half, way).start()

    def part_copy(source, index, block, target, way):
        return remote(block, target, part_send.at[source, index], part_recv.at[source, index], ways[way])

    def part(source, name):
        block = product.at[source]
        half = SUPER // 2
        if name == "far_a":
            return part_copy(source, 0, block.at[0, pl.ds(0, half)], far.at[source, 0], "x+")
        if name == "far_b":
            return part_copy(source, 1, block.at[0, pl.ds(half, half)], far.at[source, 1], "x-")
        if name == "minus_a":
            return part_copy(source, 2, block.at[0, pl.ds(2 * half, half)], near.at[source, 0], "x-")
        if name == "plus_b":
            return part_copy(source, 3, block.at[1, pl.ds(half, half)], near.at[source, 1], "x+")
        if name == "minus_b":
            return part_copy(source, 4, far.at[source, 1], near.at[source, 2], "x-")
        if name == "plus_a":
            return part_copy(source, 5, far.at[source, 0], near.at[source, 3], "x+")
        rows = pl.ds(pl.multiple_of(2 * half + (1 - y_lo) * half, half), half)
        return part_copy(source, 6, block.at[1, rows], crossed.at[source], "y")

    PARTS = ("far_a", "far_b", "minus_a", "plus_b", "minus_b", "plus_a", "cross")

    def multiply(source, half):
        landed(source, 1 - core, half)
        for which in range(2):
            def prepare(step, carry):
                rows = pl.ds(pl.multiple_of(step * 32, 32), 32)
                out = pl.ds(pl.multiple_of(which * SUPER + step * 32, 32), 32)
                high, low = split(gathered[source, which, half, rows, :])
                m_high[out, :] = high
                m_low[out, :] = low
                return carry

            lax.fori_loop(0, SUPER // 32, prepare, 0)

        def tile(step, carry):
            lanes = pl.ds(pl.multiple_of(step * 256, 256), 256)
            high = a_high[:, lanes]
            total = jnp.dot(m_low[...], high, preferred_element_type=jnp.float32)
            total += jnp.dot(m_high[...], a_low[:, lanes], preferred_element_type=jnp.float32)
            total += jnp.dot(m_high[...], high, preferred_element_type=jnp.float32)
            product[source, half, :, lanes] = total
            return carry

        lax.fori_loop(0, half_rows // 256, tile, 0)
        for name in ("far_a", "far_b", "minus_a") if half == 0 else ("plus_b",):
            part(source, name).start()

    def pass_on(source, which, half, first, arriving, leaving):
        part(source, arriving).wait_recv()
        count = SUPER // 2
        far[source, which] = far[source, which] + product[source, half, first:first + count, :]
        part(source, leaving).start()

    def own(source):
        count = SUPER // 2
        for name in ("minus_a", "plus_b", "minus_b", "plus_a"):
            part(source, name).wait_recv()
        product[source, 1, 2 * count:3 * count, :] = (
            product[source, 1, 2 * count:3 * count, :] + near[source, 0] + near[source, 3]
        )
        product[source, 1, 3 * count:, :] = product[source, 1, 3 * count:, :] + near[source, 1] + near[source, 2]
        part(source, "cross").start()

    def core_copy(source):
        where = row_at(*SOURCES[source])
        return remote(
            crossed.at[source, pl.ds(pl.multiple_of((1 - core) * SHARE, SHARE), SHARE)],
            result.at[core, pl.ds(pl.multiple_of(where * SHARE, SHARE), SHARE)],
            core_send.at[source],
            core_recv.at[where],
            ways["core"],
        )

    def pair(source):
        part(source, "cross").wait_recv()
        half = SUPER // 2
        rows = pl.ds(pl.multiple_of(2 * half + y_lo * half, half), half)
        crossed[source] = crossed[source] + product[source, 1, rows, :]
        core_copy(source).start()
        where = row_at(*SOURCES[source])
        result[core, pl.ds(pl.multiple_of(where * SHARE, SHARE), SHARE), :] = crossed[
            source, pl.ds(pl.multiple_of(core * SHARE, SHARE), SHARE), :
        ]

    for task in ORDER:
        if task[0] == "arrive":
            arrive(task[1], task[2])
        elif task[0] == "product":
            multiply(task[1], task[2])
        elif task[0] == "minus":
            pass_on(task[1], 1, 0, SUPER + SUPER // 2, "far_b", "minus_b")
        elif task[0] == "plus":
            pass_on(task[1], 0, 1, 0, "far_a", "plus_a")
        elif task[0] == "own":
            own(task[1])
        else:
            pair(task[1])

    def own_load(half):
        rows = pl.ds(pl.multiple_of(row * depth, SUPER), depth)
        return pltpu.make_async_copy(
            panel.at[rows, pl.ds(half * SUPER, SUPER)], chunk.at[half], chunk_sem.at[half]
        )

    own_load(0).start()
    own_load(1).start()
    own_load(0).wait()
    own_load(1).wait()

    def core_wait(step, carry):
        place = result.at[1 - core, pl.ds(pl.multiple_of(step * SHARE, SHARE), SHARE)]
        pltpu.make_async_copy(place, place, core_recv.at[step]).wait()
        return carry

    lax.fori_loop(0, ROWS, core_wait, 0)

    for half in range(2):
        total = jnp.zeros((SUPER, SUPER), jnp.float32)
        for block in range(blocks):
            keep = kept(row * blocks + block, col * 2 + half)
            lanes = slice(block * SUPER, (block + 1) * SUPER)
            side, first = (block * SUPER) // half_rows, (block * SUPER) % half_rows
            tile = result[side, half * SUPER:(half + 1) * SUPER, first:first + SUPER]
            off[half * SUPER:(half + 1) * SUPER, lanes] = tile * (-keep)
            t_high, t_low = split(tile)
            p_high, p_low = split(chunk[half, lanes, :] * keep)
            total += jnp.dot(t_high, p_low, preferred_element_type=jnp.float32)
            total += jnp.dot(t_low, p_high, preferred_element_type=jnp.float32)
            total += jnp.dot(t_high, p_high, preferred_element_type=jnp.float32)
        share = SUPER // ROWS
        for target in range(ROWS):
            mine[target, half] = total[target * share:(target + 1) * share]

    def diag_copy(step):
        target = lax.rem(row + step, ROWS)
        return remote(
            mine.at[target], theirs.at[step], diag_send.at[step], diag_recv.at[step], (target, col)
        )

    for step in range(1, ROWS):
        diag_copy(step).start()
    total = diag[...] + mine[row]
    for step in range(1, ROWS):
        diag_copy(step).wait_recv()
        total += theirs[step]
    diag_out[...] = total

    for step in range(1, ROWS):
        diag_copy(step).wait_send()
    for index in range(3):
        a_swap(index).wait_send()
    for message in range(len(HEAD)):
        if stays(message) is None:
            head_copy(message).wait_send()
        else:

            @pl.when(jnp.logical_not(stays(message)))
            def _():
                head_copy(message).wait_send()

    for source, half, way in SENDS:
        gather_copy(source, half, way).wait_send()
    for source in range(ROWS):
        for name in PARTS:
            part(source, name).wait_send()
        core_copy(source).wait_send()


def body(ancestor_inv, lower_panel, diag_block_inv, pattern):
    depth, width = ancestor_inv.shape
    width_here = lower_panel.shape[1]
    share = SUPER // ROWS
    half = SUPER // 2
    f32, bf16 = jnp.float32, jnp.bfloat16
    dma = pltpu.SemaphoreType.DMA
    return pl.pallas_call(
        kernel,
        out_shape=(
            jax.ShapeDtypeStruct((width_here, depth), f32),
            jax.ShapeDtypeStruct(diag_block_inv.shape, f32),
        ),
        in_specs=[
            pl.BlockSpec(memory_space=pltpu.SMEM),
            pl.BlockSpec(memory_space=pl.ANY),
            pl.BlockSpec(memory_space=pl.ANY),
            pl.BlockSpec(memory_space=pltpu.VMEM),
        ],
        out_specs=(pl.BlockSpec(memory_space=pltpu.VMEM), pl.BlockSpec(memory_space=pltpu.VMEM)),
        scratch_shapes=[
            pltpu.VMEM((ROWS, 2, 2, SUPER, depth), f32),
            pltpu.VMEM((depth, width), bf16),
            pltpu.VMEM((depth, width), bf16),
            pltpu.VMEM((2 * SUPER, depth), bf16),
            pltpu.VMEM((2 * SUPER, depth), bf16),
            pltpu.VMEM((ROWS, 2, 2 * SUPER, width), f32),
            pltpu.VMEM((ROWS, 2, half, width), f32),
            pltpu.VMEM((ROWS, 4, half, width), f32),
            pltpu.VMEM((ROWS, half, width), f32),
            pltpu.VMEM((2, width_here, width), f32),
            pltpu.VMEM((2, depth, SUPER), f32),
            pltpu.VMEM((SUPER, depth), f32),
            pltpu.VMEM((len(HEAD), SHARE, depth), f32),
            pltpu.VMEM((ROWS, 2, share, SUPER), f32),
            pltpu.VMEM((ROWS, 2, share, SUPER), f32),
            dma((2,)),
            dma((3,)),
            dma((3,)),
            dma((3,)),
            dma((len(HEAD),)),
            dma((2, 4)),
            dma((len(SENDS),)),
            dma((ROWS, 2, 2)),
            dma((ROWS, 7)),
            dma((ROWS, 7)),
            dma((ROWS,)),
            dma((ROWS,)),
            dma((ROWS,)),
            dma((ROWS,)),
        ],
        compiler_params=pltpu.CompilerParams(
            collective_id=0, has_side_effects=True, vmem_limit_bytes=63 * 2**20
        ),
        cost_estimate=pl.CostEstimate(
            flops=6 * depth * width * 16 * 2 * SUPER, bytes_accessed=16 * 2**20, transcendentals=0
        ),
    )(pattern, lower_panel, ancestor_inv, diag_block_inv)


def solution(mesh):
    in_specs = (P("row", "col"), P(None, "col"), P("col", "row", None), P())
    out_specs = (P("col", "row"), P("col", "row", None))
    return jax.shard_map(body, mesh=mesh, in_specs=in_specs, out_specs=out_specs, check_vma=False)
```

time: 592 us -> 176 us (0.30)
  waiting for transfers between devices: 330 us -> 0 us
  Pallas kernels: 0 us -> 168 us
  blocking collectives: 143 us -> 0 us
  matrix products: 69.6 us -> 0 us
  local copies, waits for them, and re-layouts: 21.2 us -> 5.41 us
  between operations: 14.1 us -> 0.64 us
  other arithmetic: 12.9 us -> 0 us
    reduce_scatter x2 -> x0, waiting for transfers between devices: 330 us -> none  [the longest x1 256 us: body(): lax.psum_scatter(lax.dot_general(relaid, ancestor_inv, (((0,), (1,)), (()...]
    pallas_call x0 -> x1, Pallas kernels: none -> 168 us  [body(): pl.pallas_call(kernel, out_shape=(jax.ShapeDtypeStruct((width_here, depth...]
    all_to_all x1 -> x0, blocking collectives: 143 us -> none  [body(): lax.all_to_all(masked, 'col', split_axis=0, concat_axis=1, tiled=True)]
    dot_general x2 -> x0, matrix products: 69.6 us -> none  [the longest x1 66 us: body(): lax.dot_general(relaid, ancestor_inv, (((0,), (1,)), ((), ())), precision...]
    all_to_all x1 -> x0, local copies, waits for them, and re-layouts: 12.6 us -> none  [body(): lax.all_to_all(masked, 'col', split_axis=0, concat_axis=1, tiled=True)]
    mul x1 -> x0, other arithmetic: 7.58 us -> none  [body(): lower_panel.reshape(block_count, SUPER, node_count, SUPER)]
    mul x3 -> x0, local copies, waits for them, and re-layouts: 6.26 us -> none  [the longest x1 4.17 us: body(): lower_panel.reshape(block_count, SUPER, node_count, SUPER)]
  transfers between devices with their start and end apart: 2 -> 0, of which waited for: 2 -> 0; matrix products, arithmetic and copies ran while one was open for 1% -> 0% of each run, Pallas kernels for 0% -> 0%
where the time goes in v4:
time: 176 us; the launch traced here: 174 us
  Pallas kernels  168 us (95%)
  local copies, waits for them, and re-layouts  5.41 us (3%)
    pallas_call x1, Pallas kernels, body(): pl.pallas_call(kernel, out_shape=(jax.ShapeDtypeStruct((width_here, depth...  168 us
    unnamed x3, local copies, waits for them, and re-layouts  5.41 us

profile of v4, /device:TPU:2, one launch (start us, length us, event | category | flops | bytes accessed | tf_op | source)
XLA Modules:
  0.0 174.0 jit_solution(5960588354291977470)
XLA Ops:
  0.6 1.4 copy.6.pattern
  2.1 168.0 %shard_map.59 = (f32[256,1536]{1,0:T(8,128)}, f32[2,16,128]{2,1,0:T(8,128)}) custom-call(s32[96,32]{1,0:T(8,128)} %copy.6.pattern, f32[12288,256]{1,0:T(8,128)} %panel.1, f32[1536,768]{1,0:T(8,128)} %ancestor.1, f32[2,16,128]{2,1,0:T(8,128)} %diag.1), custom_call_target="tpu_custom_call" | custom-call | flops 28991029248 | bytes 16777216 | tf_op jit(solution)/shard_map/pallas_call | solution.py:474
  170.0 2.7 %copy.9 = f32[256,1536]{1,0:T(8,128)} copy(f32[256,1536]{1,0:T(8,128)} %get-tuple-element.4) | data formatting | bytes 3145728
  172.7 1.3 copy.10

commit v5 on v4

--- a/solution.py
+++ b/solution.py
@@ -12,7 +12,7 @@
 SHARE = 32
 
 SOURCES = ((0, 0), (0, 1), (-1, 0), (1, 0), (-1, 1), (1, 1), (2, 0), (2, 1))
-HEAD = tuple((dx, dy, place) for dx, place in ((2, (0, 0)), (1, (1, 0)), (-1, (0, 1)), (0, (1, 1))) for dy in range(2))
+HEAD = tuple((dx, dy, place) for dx, place in ((2, (0, 0)), (0, (1, 0)), (1, (0, 1)), (-1, (1, 1))) for dy in range(2))
 
 
 def forwards(source, half):
@@ -38,71 +38,90 @@
             SENDS[(_source, _half, _way)] = len(SENDS)
 
 ORDER = (
+    ("convert", 0),
     ("arrive", 0, 0),
+    ("convert", 1),
     ("arrive", 0, 1),
     ("product", 0, 0),
     ("product", 0, 1),
-    ("minus", 0),
-    ("plus", 0),
+    ("minus", 0, 0),
+    ("plus", 0, 0),
     ("arrive", 2, 0),
     ("arrive", 3, 0),
     ("arrive", 1, 0),
-    ("own", 0),
+    ("own", 0, 0),
     ("product", 2, 0),
     ("product", 3, 0),
     ("product", 1, 0),
-    ("minus", 2),
-    ("pair", 0),
+    ("pair", 0, 0),
     ("arrive", 2, 1),
     ("arrive", 3, 1),
     ("arrive", 1, 1),
     ("product", 2, 1),
-    ("minus", 3),
-    ("plus", 2),
+    ("minus", 2, 0),
+    ("plus", 2, 0),
     ("product", 3, 1),
-    ("plus", 3),
+    ("minus", 3, 0),
+    ("plus", 3, 0),
     ("product", 1, 1),
-    ("minus", 1),
-    ("plus", 1),
+    ("minus", 1, 0),
+    ("plus", 1, 0),
     ("arrive", 5, 0),
     ("arrive", 6, 0),
+    ("own", 2, 0),
     ("product", 5, 0),
     ("product", 6, 0),
-    ("own", 2),
-    ("own", 3),
+    ("own", 3, 0),
+    ("pair", 2, 0),
+    ("first", 5, 0),
     ("arrive", 4, 0),
     ("arrive", 6, 1),
-    ("pair", 2),
-    ("minus", 5),
-    ("own", 1),
-    ("pair", 3),
+    ("first", 5, 1),
+    ("own", 1, 0),
     ("product", 4, 0),
+    ("pair", 3, 0),
     ("product", 6, 1),
-    ("minus", 6),
-    ("plus", 6),
-    ("pair", 1),
+    ("minus", 6, 0),
+    ("plus", 6, 0),
+    ("pair", 1, 0),
+    ("first", 4, 0),
     ("arrive", 4, 1),
     ("arrive", 5, 1),
+    ("first", 4, 1),
     ("product", 4, 1),
-    ("minus", 4),
-    ("plus", 4),
+    ("own", 6, 0),
     ("product", 5, 1),
-    ("plus", 5),
-    ("own", 6),
+    ("first", 4, 2),
+    ("minus", 4, 0),
     ("arrive", 7, 0),
-    ("own", 4),
+    ("first", 4, 3),
     ("arrive", 7, 1),
-    ("pair", 6),
+    ("plus", 4, 0),
     ("product", 7, 0),
+    ("pair", 6, 0),
     ("product", 7, 1),
-    ("own", 5),
-    ("pair", 4),
-    ("minus", 7),
-    ("plus", 7),
-    ("pair", 5),
-    ("own", 7),
-    ("pair", 7),
+    ("minus", 7, 0),
+    ("plus", 7, 0),
+    ("own", 4, 0),
+    ("minus", 7, 1),
+    ("plus", 7, 1),
+    ("first", 5, 2),
+    ("minus", 5, 0),
+    ("minus", 7, 2),
+    ("plus", 7, 2),
+    ("first", 5, 3),
+    ("plus", 5, 0),
+    ("own", 7, 0),
+    ("own", 7, 1),
+    ("pair", 7, 0),
+    ("pair", 7, 1),
+    ("own", 7, 2),
+    ("own", 5, 0),
+    ("pair", 7, 2),
 )
+TILES = (1, 1, 1, 1, 1, 1, 1, 3)
+PAIR_FIRST = (4, 5)
+PARTS = ("far_a", "far_b", "minus_a", "plus_b", "minus_b", "plus_a", "cross")
 
 
 def split(value):
@@ -113,8 +132,8 @@
 
 def kernel(
     pattern, panel, ancestor, diag, off, diag_out,
-    gathered, a_high, a_low, m_high, m_low, product, far, near, crossed, result, chunk, turned, pieces, mine, theirs,
-    chunk_sem, a_sem, a_send, a_recv, head_send, head_recv, gather_send, gather_recv, part_send, part_recv,
+    gathered, a_high, a_low, m_high, m_low, product, far, near, crossed, paired, result, chunk, turned, pieces, mine, theirs,
+    chunk_sem, a_sem, a_send, a_recv, head_send, head_recv, gather_send, gather_recv, part_send, part_recv, pair_send, pair_recv,
     core_send, core_recv, diag_send, diag_recv,
 ):
     row, col = lax.axis_index("row"), lax.axis_index("col")
@@ -252,6 +271,15 @@
             def _():
                 head_copy(message).start()
 
+    def own_load(half):
+        rows = pl.ds(pl.multiple_of(row * depth, SUPER), depth)
+        return pltpu.make_async_copy(
+            panel.at[rows, pl.ds(half * SUPER, SUPER)], chunk.at[half], chunk_sem.at[half]
+        )
+
+    own_load(0).start()
+    own_load(1).start()
+
     def convert(place, part, offset):
         slot, half = place[part]
         for step in range(2):
@@ -263,18 +291,20 @@
                 a_high[rows, lanes] = high
                 a_low[rows, lanes] = low
 
-    for part in range(3):
-        a_load(part).wait()
-        convert(own_place, part, core * cols_here)
-    for part in range(3):
-        a_swap(part).wait_recv()
-        convert(other_place, part, (1 - core) * cols_here)
-
-    def gather_copy(source, half, way):
+    def convert_all(swapped):
+        for part in range(3):
+            if swapped:
+                a_swap(part).wait_recv()
+                convert(other_place, part, (1 - core) * cols_here)
+            else:
+                a_load(part).wait()
+                convert(own_place, part, core * cols_here)
+
+    def gather_copy(source, half, way, rows=slice(None)):
         target = dict(forwards(source, half))[way]
         return remote(
-            gathered.at[source, core, half],
-            gathered.at[target, core, half],
+            gathered.at[source, core, half, rows],
+            gathered.at[target, core, half, rows],
             gather_send.at[SENDS[(source, half, way)]],
             gather_recv.at[target, core, half],
             ways[way],
@@ -285,37 +315,79 @@
         pltpu.make_async_copy(place, place, gather_recv.at[source, which, half]).wait()
 
     def arrive(source, half):
-        if source == 0:
-            for piece in range(4):
-                place = gathered.at[0, core, half, pl.ds(piece * SHARE, SHARE)]
-                pltpu.make_async_copy(place, place, head_recv.at[half, piece]).wait()
-        else:
+        if source > 0:
             landed(source, core, half)
-        for way, _ in forwards(source, half):
-            gather_copy(source, half, way).start()
-
-    def part_copy(source, index, block, target, way):
-        return remote(block, target, part_send.at[source, index], part_recv.at[source, index], ways[way])
-
-    def part(source, name):
-        block = product.at[source]
+            for way, _ in forwards(source, half):
+                gather_copy(source, half, way).start()
+            return
+        for step in range(4):
+            piece = ((1 - y_lo) if step >= 2 else y_lo) * 2 + step % 2
+            rows = pl.ds(pl.multiple_of(piece * SHARE, SHARE), SHARE)
+            place = gathered.at[0, core, half, rows]
+            pltpu.make_async_copy(place, place, head_recv.at[half, piece]).wait()
+            for way, _ in forwards(source, half):
+                gather_copy(source, half, way, rows).start()
+
+    def tiles(source):
+        count = TILES[source]
+        return [slice(t * half_rows // count, (t + 1) * half_rows // count) for t in range(count)]
+
+    def part(source, name, tile=None):
+        lanes = slice(None) if tile is None else tiles(source)[tile]
+        index = PARTS.index(name)
         half = SUPER // 2
-        if name == "far_a":
-            return part_copy(source, 0, block.at[0, pl.ds(0, half)], far.at[source, 0], "x+")
-        if name == "far_b":
-            return part_copy(source, 1, block.at[0, pl.ds(half, half)], far.at[source, 1], "x-")
-        if name == "minus_a":
-            return part_copy(source, 2, block.at[0, pl.ds(2 * half, half)], near.at[source, 0], "x-")
-        if name == "plus_b":
-            return part_copy(source, 3, block.at[1, pl.ds(half, half)], near.at[source, 1], "x+")
-        if name == "minus_b":
-            return part_copy(source, 4, far.at[source, 1], near.at[source, 2], "x-")
-        if name == "plus_a":
-            return part_copy(source, 5, far.at[source, 0], near.at[source, 3], "x+")
-        rows = pl.ds(pl.multiple_of(2 * half + (1 - y_lo) * half, half), half)
-        return part_copy(source, 6, block.at[1, rows], crossed.at[source], "y")
-
-    PARTS = ("far_a", "far_b", "minus_a", "plus_b", "minus_b", "plus_a", "cross")
+        if source in PAIR_FIRST:
+            count = half // 2
+            held = paired.at[PAIR_FIRST.index(source)]
+            block, target, way = {
+                "far_a": lambda: (held.at[0, pl.ds(0, count)], far.at[source, 0, pl.ds(0, count)], "x+"),
+                "far_b": lambda: (held.at[0, pl.ds(count, count)], far.at[source, 1, pl.ds(0, count)], "x-"),
+                "minus_a": lambda: (held.at[2, pl.ds(0, count)], near.at[source, 0, pl.ds(0, count)], "x-"),
+                "plus_b": lambda: (held.at[3, pl.ds(count, count)], near.at[source, 1, pl.ds(0, count)], "x+"),
+                "minus_b": lambda: (far.at[source, 1, pl.ds(0, count)], near.at[source, 2, pl.ds(0, count)], "x-"),
+                "plus_a": lambda: (far.at[source, 0, pl.ds(0, count)], near.at[source, 3, pl.ds(0, count)], "x+"),
+            }[name]()
+            return remote(
+                block, target, part_send.at[source, index], part_recv.at[source, index, 0], ways[way]
+            )
+        first, second = product.at[source, 0], product.at[source, 1]
+        block, target, way = {
+            "far_a": lambda: (first.at[pl.ds(0, half), lanes], far.at[source, 0, :, lanes], "x+"),
+            "far_b": lambda: (first.at[pl.ds(half, half), lanes], far.at[source, 1, :, lanes], "x-"),
+            "minus_a": lambda: (second.at[pl.ds(0, half), lanes], near.at[source, 0, :, lanes], "x-"),
+            "plus_b": lambda: (second.at[pl.ds(3 * half, half), lanes], near.at[source, 1, :, lanes], "x+"),
+            "minus_b": lambda: (far.at[source, 1, :, lanes], near.at[source, 2, :, lanes], "x-"),
+            "plus_a": lambda: (far.at[source, 0, :, lanes], near.at[source, 3, :, lanes], "x+"),
+            "cross": lambda: (
+                first.at[pl.ds(pl.multiple_of(2 * half + (1 - y_lo) * half, half), half), lanes],
+                crossed.at[source, :, lanes],
+                "y",
+            ),
+        }[name]()
+        return remote(
+            block, target, part_send.at[source, index], part_recv.at[source, index, tile or 0], ways[way]
+        )
+
+    def pair_copy(source, unit):
+        half = SUPER // 2
+        rows = pl.ds(pl.multiple_of((unit % 2) * SUPER + (1 - y_lo) * half, half), half)
+        place = PAIR_FIRST.index(source)
+        return remote(
+            product.at[source, unit // 2, rows],
+            paired.at[place, unit],
+            pair_send.at[place, unit],
+            pair_recv.at[place, unit],
+            ways["y"],
+        )
+
+    def pair_first(source, unit):
+        pair_copy(source, unit).wait_recv()
+        half = SUPER // 2
+        rows = pl.ds(pl.multiple_of((unit % 2) * SUPER + y_lo * half, half), half)
+        place = PAIR_FIRST.index(source)
+        paired[place, unit] = paired[place, unit] + product[source, unit // 2, rows, :]
+        for name in (("far_a", "far_b"), (), ("minus_a",), ("plus_b",))[unit]:
+            part(source, name, 0).start()
 
     def multiply(source, half):
         landed(source, 1 - core, half)
@@ -340,68 +412,92 @@
             return carry
 
         lax.fori_loop(0, half_rows // 256, tile, 0)
-        for name in ("far_a", "far_b", "minus_a") if half == 0 else ("plus_b",):
-            part(source, name).start()
-
-    def pass_on(source, which, half, first, arriving, leaving):
-        part(source, arriving).wait_recv()
+        if source in PAIR_FIRST:
+            for unit in (2 * half, 2 * half + 1):
+                pair_copy(source, unit).start()
+            return
+        for index in range(TILES[source]):
+            for name in ("far_a", "far_b") if half == 0 else ("minus_a", "plus_b"):
+                part(source, name, index).start()
+
+    def pass_on(source, tile, which, first, arriving, leaving):
+        part(source, arriving, tile).wait_recv()
         count = SUPER // 2
-        far[source, which] = far[source, which] + product[source, half, first:first + count, :]
-        part(source, leaving).start()
-
-    def own(source):
+        lanes = tiles(source)[tile]
+        if source in PAIR_FIRST:
+            count = count // 2
+            unit, start = ((3, 0), (2, count))[which]
+            far[source, which, :count] = far[source, which, :count] + paired[
+                PAIR_FIRST.index(source), unit, start:start + count
+            ]
+            part(source, leaving, tile).start()
+            return
+        far[source, which, :, lanes] = far[source, which, :, lanes] + product[source, 1, first:first + count, lanes]
+        part(source, leaving, tile).start()
+
+    def own(source, tile):
         count = SUPER // 2
+        lanes = tiles(source)[tile]
         for name in ("minus_a", "plus_b", "minus_b", "plus_a"):
-            part(source, name).wait_recv()
-        product[source, 1, 2 * count:3 * count, :] = (
-            product[source, 1, 2 * count:3 * count, :] + near[source, 0] + near[source, 3]
-        )
-        product[source, 1, 3 * count:, :] = product[source, 1, 3 * count:, :] + near[source, 1] + near[source, 2]
-        part(source, "cross").start()
-
-    def core_copy(source):
+            part(source, name, tile).wait_recv()
+        if source in PAIR_FIRST:
+            count = count // 2
+            place = PAIR_FIRST.index(source)
+            for first, one, two in ((0, 0, 3), (count, 1, 2)):
+                crossed[source, first:first + count] = (
+                    paired[place, 1, first:first + count] + near[source, one, :count] + near[source, two, :count]
+                )
+            hand_over(source, lanes)
+            return
+        for first, one, two in ((2 * count, 0, 3), (3 * count, 1, 2)):
+            product[source, 0, first:first + count, lanes] = (
+                product[source, 0, first:first + count, lanes] + near[source, one, :, lanes] + near[source, two, :, lanes]
+            )
+        part(source, "cross", tile).start()
+
+    def core_copy(source, lanes=slice(None)):
         where = row_at(*SOURCES[source])
         return remote(
-            crossed.at[source, pl.ds(pl.multiple_of((1 - core) * SHARE, SHARE), SHARE)],
-            result.at[core, pl.ds(pl.multiple_of(where * SHARE, SHARE), SHARE)],
+            crossed.at[source, pl.ds(pl.multiple_of((1 - core) * SHARE, SHARE), SHARE), lanes],
+            result.at[core, pl.ds(pl.multiple_of(where * SHARE, SHARE), SHARE), lanes],
             core_send.at[source],
             core_recv.at[where],
             ways["core"],
         )
 
-    def pair(source):
-        part(source, "cross").wait_recv()
+    def pair(source, tile):
+        part(source, "cross", tile).wait_recv()
+        lanes = tiles(source)[tile]
         half = SUPER // 2
         rows = pl.ds(pl.multiple_of(2 * half + y_lo * half, half), half)
-        crossed[source] = crossed[source] + product[source, 1, rows, :]
-        core_copy(source).start()
+        crossed[source, :, lanes] = crossed[source, :, lanes] + product[source, 0, rows, lanes]
+        hand_over(source, lanes)
+
+    def hand_over(source, lanes):
+        core_copy(source, lanes).start()
         where = row_at(*SOURCES[source])
-        result[core, pl.ds(pl.multiple_of(where * SHARE, SHARE), SHARE), :] = crossed[
-            source, pl.ds(pl.multiple_of(core * SHARE, SHARE), SHARE), :
+        result[core, pl.ds(pl.multiple_of(where * SHARE, SHARE), SHARE), lanes] = crossed[
+            source, pl.ds(pl.multiple_of(core * SHARE, SHARE), SHARE), lanes
         ]
 
     for task in ORDER:
         if task[0] == "arrive":
             arrive(task[1], task[2])
+        elif task[0] == "convert":
+            convert_all(task[1] == 1)
         elif task[0] == "product":
             multiply(task[1], task[2])
         elif task[0] == "minus":
-            pass_on(task[1], 1, 0, SUPER + SUPER // 2, "far_b", "minus_b")
+            pass_on(task[1], task[2], 1, SUPER // 2, "far_b", "minus_b")
         elif task[0] == "plus":
-            pass_on(task[1], 0, 1, 0, "far_a", "plus_a")
+            pass_on(task[1], task[2], 0, SUPER, "far_a", "plus_a")
+        elif task[0] == "first":
+            pair_first(task[1], task[2])
         elif task[0] == "own":
-            own(task[1])
+            own(task[1], task[2])
         else:
-            pair(task[1])
-
-    def own_load(half):
-        rows = pl.ds(pl.multiple_of(row * depth, SUPER), depth)
-        return pltpu.make_async_copy(
-            panel.at[rows, pl.ds(half * SUPER, SUPER)], chunk.at[half], chunk_sem.at[half]
-        )
-
-    own_load(0).start()
-    own_load(1).start()
+            pair(task[1], task[2])
+
     own_load(0).wait()
     own_load(1).wait()
 
@@ -412,16 +508,16 @@
 
     lax.fori_loop(0, ROWS, core_wait, 0)
 
+    def tile_of(half, block):
+        side, first = (block * SUPER) // half_rows, (block * SUPER) % half_rows
+        return result[side, half * SUPER:(half + 1) * SUPER, first:first + SUPER]
+
     for half in range(2):
         total = jnp.zeros((SUPER, SUPER), jnp.float32)
         for block in range(blocks):
-            keep = kept(row * blocks + block, col * 2 + half)
             lanes = slice(block * SUPER, (block + 1) * SUPER)
-            side, first = (block * SUPER) // half_rows, (block * SUPER) % half_rows
-            tile = result[side, half * SUPER:(half + 1) * SUPER, first:first + SUPER]
-            off[half * SUPER:(half + 1) * SUPER, lanes] = tile * (-keep)
-            t_high, t_low = split(tile)
-            p_high, p_low = split(chunk[half, lanes, :] * keep)
+            t_high, t_low = split(tile_of(half, block))
+            p_high, p_low = split(chunk[half, lanes, :] * kept(row * blocks + block, col * 2 + half))
             total += jnp.dot(t_high, p_low, preferred_element_type=jnp.float32)
             total += jnp.dot(t_low, p_high, preferred_element_type=jnp.float32)
             total += jnp.dot(t_high, p_high, preferred_element_type=jnp.float32)
@@ -437,14 +533,11 @@
 
     for step in range(1, ROWS):
         diag_copy(step).start()
-    total = diag[...] + mine[row]
-    for step in range(1, ROWS):
-        diag_copy(step).wait_recv()
-        total += theirs[step]
-    diag_out[...] = total
-
-    for step in range(1, ROWS):
-        diag_copy(step).wait_send()
+
+    for half in range(2):
+        for block in range(blocks):
+            keep = kept(row * blocks + block, col * 2 + half)
+            off[half * SUPER:(half + 1) * SUPER, block * SUPER:(block + 1) * SUPER] = tile_of(half, block) * (-keep)
     for index in range(3):
         a_swap(index).wait_send()
     for message in range(len(HEAD)):
@@ -459,9 +552,20 @@
     for source, half, way in SENDS:
         gather_copy(source, half, way).wait_send()
     for source in range(ROWS):
-        for name in PARTS:
+        for name in PARTS[:6] if source in PAIR_FIRST else PARTS:
             part(source, name).wait_send()
+        if source in PAIR_FIRST:
+            for unit in range(4):
+                pair_copy(source, unit).wait_send()
         core_copy(source).wait_send()
+
+    total = diag[...] + mine[row]
+    for step in range(1, ROWS):
+        diag_copy(step).wait_recv()
+        total += theirs[step]
+    diag_out[...] = total
+    for step in range(1, ROWS):
+        diag_copy(step).wait_send()
 
 
 def body(ancestor_inv, lower_panel, diag_block_inv, pattern):
@@ -494,6 +598,7 @@
             pltpu.VMEM((ROWS, 2, half, width), f32),
             pltpu.VMEM((ROWS, 4, half, width), f32),
             pltpu.VMEM((ROWS, half, width), f32),
+            pltpu.VMEM((len(PAIR_FIRST), 4, half, width), f32),
             pltpu.VMEM((2, width_here, width), f32),
             pltpu.VMEM((2, depth, SUPER), f32),
             pltpu.VMEM((SUPER, depth), f32),
@@ -509,7 +614,9 @@
             dma((len(SENDS),)),
             dma((ROWS, 2, 2)),
             dma((ROWS, 7)),
-            dma((ROWS, 7)),
+            dma((ROWS, 7, 3)),
+            dma((len(PAIR_FIRST), 4)),
+            dma((len(PAIR_FIRST), 4)),
             dma((ROWS,)),
             dma((ROWS,)),
             dma((ROWS,)),

time: 176 us -> 172 us (0.977)
  Pallas kernels: 168 us -> 164 us
    pallas_call x1, Pallas kernels: 168 us -> 164 us  [body(): pl.pallas_call(kernel, out_shape=(jax.ShapeDtypeStruct((width_here, depth...]
where the time goes in v5:
time: 172 us; the launch traced here: 170 us
  Pallas kernels  164 us (95%)
  local copies, waits for them, and re-layouts  5.41 us (3%)
    pallas_call x1, Pallas kernels, body(): pl.pallas_call(kernel, out_shape=(jax.ShapeDtypeStruct((width_here, depth...  164 us
    unnamed x3, local copies, waits for them, and re-layouts  5.41 us

profile of v5, /device:TPU:2, one launch (start us, length us, event | category | flops | bytes accessed | tf_op | source)
XLA Modules:
  0.0 170.2 jit_solution(6319906447434460027)
XLA Ops:
  0.6 1.4 copy.6.pattern
  2.1 164.1 %shard_map.59 = (f32[256,1536]{1,0:T(8,128)}, f32[2,16,128]{2,1,0:T(8,128)}) custom-call(s32[96,32]{1,0:T(8,128)} %copy.6.pattern, f32[12288,256]{1,0:T(8,128)} %panel.1, f32[1536,768]{1,0:T(8,128)} %ancestor.1, f32[2,16,128]{2,1,0:T(8,128)} %diag.1), custom_call_target="tpu_custom_call" | custom-call | flops 28991029248 | bytes 16777216 | tf_op jit(solution)/shard_map/pallas_call | solution.py:578
  166.2 2.7 %copy.9 = f32[256,1536]{1,0:T(8,128)} copy(f32[256,1536]{1,0:T(8,128)} %get-tuple-element.4) | data formatting | bytes 3145728
  168.9 1.3 copy.10

commit v6 on v5

--- a/solution.py
+++ b/solution.py
@@ -39,9 +39,8 @@
 
 ORDER = (
     ("convert", 0),
-    ("arrive", 0, 0),
+    ("rest", 1),
     ("convert", 1),
-    ("arrive", 0, 1),
     ("product", 0, 0),
     ("product", 0, 1),
     ("minus", 0, 0),
@@ -131,10 +130,11 @@
 
 
 def kernel(
-    pattern, panel, ancestor, diag, off, diag_out,
+    pattern_in, panel, ancestor, diag, off, diag_out,
+    pattern,
     gathered, a_high, a_low, m_high, m_low, product, far, near, crossed, paired, result, chunk, turned, pieces, mine, theirs,
     chunk_sem, a_sem, a_send, a_recv, head_send, head_recv, gather_send, gather_recv, part_send, part_recv, pair_send, pair_recv,
-    core_send, core_recv, diag_send, diag_recv,
+    core_send, core_recv, diag_send, diag_recv, pattern_sem,
 ):
     row, col = lax.axis_index("row"), lax.axis_index("col")
     y_hi, z = row // RING, lax.rem(row, RING)
@@ -168,6 +168,9 @@
             src_ref=source, dst_ref=target, send_sem=send, recv_sem=recv, device_id=device, device_id_type=MESH
         )
 
+    pattern_copy = pltpu.make_async_copy(pattern_in, pattern, pattern_sem)
+    pattern_copy.start()
+
     barrier = pltpu.get_barrier_semaphore()
 
     def greet(device):
@@ -252,6 +255,38 @@
             chunk_load(message + 2).start()
         pieces[message] = turned[pl.ds(pl.multiple_of(lax.rem(row, 4) * SHARE, SHARE), SHARE), :]
 
+    def gather_copy(source, half, way, rows=slice(None)):
+        target = dict(forwards(source, half))[way]
+        return remote(
+            gathered.at[source, core, half, rows],
+            gathered.at[target, core, half, rows],
+            gather_send.at[SENDS[(source, half, way)]],
+            gather_recv.at[target, core, half],
+            ways[way],
+        )
+
+    def landed(source, which, half):
+        place = gathered.at[source, which, half]
+        pltpu.make_async_copy(place, place, gather_recv.at[source, which, half]).wait()
+
+    def arrive(source, half):
+        if source > 0:
+            landed(source, core, half)
+            for way, _ in forwards(source, half):
+                gather_copy(source, half, way).start()
+            return
+        first_sends(half, (0, 1, 2, 3))
+
+    def first_sends(half, steps):
+        for step in steps:
+            piece = ((1 - y_lo) if step >= 2 else y_lo) * 2 + step % 2
+            rows = pl.ds(pl.multiple_of(piece * SHARE, SHARE), SHARE)
+            place = gathered.at[0, core, half, rows]
+            pltpu.make_async_copy(place, place, head_recv.at[half, piece]).wait()
+            for way, _ in forwards(0, half):
+                gather_copy(0, half, way, rows).start()
+
+    pattern_copy.wait()
     turn(0)
     pl.semaphore_wait(barrier, 18)
     for part in range(3):
@@ -271,6 +306,11 @@
             def _():
                 head_copy(message).start()
 
+        if message == 3:
+            first_sends(0, (0, 1))
+        if message == 7:
+            first_sends(0, (2, 3))
+
     def own_load(half):
         rows = pl.ds(pl.multiple_of(row * depth, SUPER), depth)
         return pltpu.make_async_copy(
@@ -299,34 +339,6 @@
             else:
                 a_load(part).wait()
                 convert(own_place, part, core * cols_here)
-
-    def gather_copy(source, half, way, rows=slice(None)):
-        target = dict(forwards(source, half))[way]
-        return remote(
-            gathered.at[source, core, half, rows],
-            gathered.at[target, core, half, rows],
-            gather_send.at[SENDS[(source, half, way)]],
-            gather_recv.at[target, core, half],
-            ways[way],
-        )
-
-    def landed(source, which, half):
-        place = gathered.at[source, which, half]
-        pltpu.make_async_copy(place, place, gather_recv.at[source, which, half]).wait()
-
-    def arrive(source, half):
-        if source > 0:
-            landed(source, core, half)
-            for way, _ in forwards(source, half):
-                gather_copy(source, half, way).start()
-            return
-        for step in range(4):
-            piece = ((1 - y_lo) if step >= 2 else y_lo) * 2 + step % 2
-            rows = pl.ds(pl.multiple_of(piece * SHARE, SHARE), SHARE)
-            place = gathered.at[0, core, half, rows]
-            pltpu.make_async_copy(place, place, head_recv.at[half, piece]).wait()
-            for way, _ in forwards(source, half):
-                gather_copy(source, half, way, rows).start()
 
     def tiles(source):
         count = TILES[source]
@@ -483,6 +495,8 @@
     for task in ORDER:
         if task[0] == "arrive":
             arrive(task[1], task[2])
+        elif task[0] == "rest":
+            first_sends(1, (0, 1, 2, 3))
         elif task[0] == "convert":
             convert_all(task[1] == 1)
         elif task[0] == "product":
@@ -582,13 +596,14 @@
             jax.ShapeDtypeStruct(diag_block_inv.shape, f32),
         ),
         in_specs=[
-            pl.BlockSpec(memory_space=pltpu.SMEM),
+            pl.BlockSpec(memory_space=pl.ANY),
             pl.BlockSpec(memory_space=pl.ANY),
             pl.BlockSpec(memory_space=pl.ANY),
             pl.BlockSpec(memory_space=pltpu.VMEM),
         ],
         out_specs=(pl.BlockSpec(memory_space=pltpu.VMEM), pl.BlockSpec(memory_space=pltpu.VMEM)),
         scratch_shapes=[
+            pltpu.SMEM(pattern.shape, pattern.dtype),
             pltpu.VMEM((ROWS, 2, 2, SUPER, depth), f32),
             pltpu.VMEM((depth, width), bf16),
             pltpu.VMEM((depth, width), bf16),
@@ -621,6 +636,7 @@
             dma((ROWS,)),
             dma((ROWS,)),
             dma((ROWS,)),
+            dma,
         ],
         compiler_params=pltpu.CompilerParams(
             collective_id=0, has_side_effects=True, vmem_limit_bytes=63 * 2**20

time: 172 us -> 171 us (level)
  no operation moved by 1% of the time
where the time goes in v6:
time: 171 us; the launch traced here: 169 us
  Pallas kernels  163 us (95%)
  local copies, waits for them, and re-layouts  5.41 us (3%)
    pallas_call x1, Pallas kernels, body(): pl.pallas_call(kernel, out_shape=(jax.ShapeDtypeStruct((width_here, depth...  163 us
    unnamed x3, local copies, waits for them, and re-layouts  5.41 us

profile of v6, /device:TPU:2, one launch (start us, length us, event | category | flops | bytes accessed | tf_op | source)
XLA Modules:
  0.0 168.6 jit_solution(16347610221823141459)
XLA Ops:
  0.6 1.4 copy.6.pattern_in
  2.1 162.5 %shard_map.59 = (f32[256,1536]{1,0:T(8,128)}, f32[2,16,128]{2,1,0:T(8,128)}) custom-call(s32[96,32]{1,0:T(8,128)} %copy.6.pattern_in, f32[12288,256]{1,0:T(8,128)} %panel.1, f32[1536,768]{1,0:T(8,128)} %ancestor.1, f32[2,16,128]{2,1,0:T(8,128)} %diag.1), custom_call_target="tpu_custom_call" | custom-call | flops 28991029248 | bytes 16777216 | tf_op jit(solution)/shard_map/pallas_call | solution.py:592
  164.6 2.7 %copy.9 = f32[256,1536]{1,0:T(8,128)} copy(f32[256,1536]{1,0:T(8,128)} %get-tuple-element.4) | data formatting | bytes 3145728
  167.3 1.3 copy.10

commit v7 on v6

--- a/solution.py
+++ b/solution.py
@@ -250,7 +250,7 @@
             turned[:, rows] = tile.T
             return carry
 
-        lax.fori_loop(0, blocks, block_turn, 0, unroll=2)
+        lax.fori_loop(0, blocks, block_turn, 0, unroll=6)
         if message + 2 < len(HEAD):
             chunk_load(message + 2).start()
         pieces[message] = turned[pl.ds(pl.multiple_of(lax.rem(row, 4) * SHARE, SHARE), SHARE), :]
@@ -412,7 +412,7 @@
                 m_low[out, :] = low
                 return carry
 
-            lax.fori_loop(0, SUPER // 32, prepare, 0)
+            lax.fori_loop(0, SUPER // 32, prepare, 0, unroll=2)
 
         def tile(step, carry):
             lanes = pl.ds(pl.multiple_of(step * 256, 256), 256)

time: 171 us -> 171 us (level)
  no operation moved by 1% of the time
where the time goes in v7:
time: 171 us; the launch traced here: 168 us
  Pallas kernels  162 us (95%)
  local copies, waits for them, and re-layouts  5.41 us (3%)
    pallas_call x1, Pallas kernels, body(): pl.pallas_call(kernel, out_shape=(jax.ShapeDtypeStruct((width_here, depth...  162 us
    unnamed x3, local copies, waits for them, and re-layouts  5.41 us

profile of v7, /device:TPU:2, one launch (start us, length us, event | category | flops | bytes accessed | tf_op | source)
XLA Modules:
  0.0 168.0 jit_solution(5327835098950829646)
XLA Ops:
  0.6 1.4 copy.6.pattern_in
  2.1 162.0 %shard_map.59 = (f32[256,1536]{1,0:T(8,128)}, f32[2,16,128]{2,1,0:T(8,128)}) custom-call(s32[96,32]{1,0:T(8,128)} %copy.6.pattern_in, f32[12288,256]{1,0:T(8,128)} %panel.1, f32[1536,768]{1,0:T(8,128)} %ancestor.1, f32[2,16,128]{2,1,0:T(8,128)} %diag.1), custom_call_target="tpu_custom_call" | custom-call | flops 28991029248 | bytes 16777216 | tf_op jit(solution)/shard_map/pallas_call | solution.py:592
  164.0 2.7 %copy.9 = f32[256,1536]{1,0:T(8,128)} copy(f32[256,1536]{1,0:T(8,128)} %get-tuple-element.4) | data formatting | bytes 3145728
  166.7 1.3 copy.10
